TPU v7x, 32 devices: a whole 2x2x4 slice. The times are simulated.
32 devices in a mesh: cases: 2 (over y), circ: 4 (over x, core), lat: 4 (over z).
Axes of the slice: x: 2, y: 2, z: 4, core: 2. Of those that a mesh axis runs over, the one named last changes fastest.
Arguments:
- disp: float32 [3, 1024, 512], P(None, ('cases', 'circ'), 'lat'), parts along dimension 1, may hold values from -6 to 6
- stiff: float32 [2, 1024, 512], P(None, ('cases', 'circ'), 'lat'), parts along dimension 1, may hold values from 1 to 4
- spin: float32 [2], P('cases'), parts along dimension 0, may hold values from 0.2 to 0.8
- load: float32 [3, 1024, 512], P(None, ('cases', 'circ'), 'lat'), parts along dimension 1, may hold values from -6 to 6
- foot_node: int32 [32768], P(('cases', 'circ', 'lat')), parts along dimension 0, may hold values from 0 to 16383, as said below
- foot_dest: int32 [32768], P(('cases', 'circ', 'lat')), parts along dimension 0, may hold values from 0 to 15, as said below
- foot_slot: int32 [32768], P(('cases', 'circ', 'lat')), parts along dimension 0, may hold values from 0 to 511
- foot_count: int32 [32], P(('cases', 'circ', 'lat')), parts along dimension 0, may hold values from 0 to 1024, as said below
- road: float32 [16384], P(('cases', 'circ', 'lat')), parts along dimension 0, may hold values from -6 to 6
- active: int32 [16384], P(('cases', 'circ', 'lat')), parts along dimension 0, may hold values 0 or 1
- influence: float32 [32, 512, 512], P(('cases', 'circ', 'lat')), parts along dimension 0, may hold values from 0 to 4, as said below
Outputs:
- new_disp: float32 [3, 1024, 512], P(None, ('cases', 'circ'), 'lat'), parts along dimension 1
- pressure: float32 [16384], P(('cases', 'circ', 'lat')), parts along dimension 0
There are 2 independent parts, one for each index of `cases`. A program takes and returns all parts, laid end to end along the dimension named above; each array names one. Nothing has to cross between parts.
Inputs may be any that keep to these rules, and one draw needn't show every extreme that they name: Rows past a device's foot_count are ignored; among live rows every pair (foot_dest, foot_slot) occurs exactly once over all devices, so each patch receives exactly 512 rows; at most 128 live rows go from one device to one owner, and some device sends exactly 128 to some owner. `foot_node`: a device's live rows name distinct nodes. `foot_count`: counts sum to 8192. `influence`: symmetric positive definite.
All inputs are finite; a program needn't handle non-finite values. No bound on the sum of `active` on one device may be relied on, other than what follows from the above.
Results may differ from a plain program's by a relative error of at most 0.00002.
Values sent between devices are 32-bit elements; how exact they have to be, the bound alone decides.
No kernel may reach another device: no remote copies, remote signals or barrier semaphores. Data moves between devices by JAX's collectives and lax.ppermute only.
A program may use at most 128 MiB of HBM per device.

v0:
```python
import jax
import jax.numpy as jnp
from jax import lax
from jax.sharding import PartitionSpec as P


def with_halo(cells, sides, width, closed):
    for axis, dim in sides:
        count = lax.axis_size(axis)
        ends = count if closed else count - 1
        head = lax.slice_in_dim(cells, 0, width, axis=dim)
        tail = lax.slice_in_dim(cells, cells.shape[dim] - width, cells.shape[dim], axis=dim)
        cells = jnp.concatenate(
            [
                lax.ppermute(tail, axis, [(i, (i + 1) % count) for i in range(ends)]),
                cells,
                lax.ppermute(head, axis, [((i + 1) % count, i) for i in range(ends)]),
            ],
            axis=dim,
        )
    return cells


def solve_patch(patch_w, patch_k, road, active, block):
    size = patch_w.shape[0]
    mask = active.astype(jnp.float32)
    eye = jnp.eye(size, dtype=jnp.float32)
    g_mat = block + eye * (1.0 / patch_k)[:, None]
    g_act = mask[:, None] * mask[None, :] * g_mat + eye * (1.0 - mask)[:, None]
    rhs = (mask * (patch_w - road))[:, None]
    factor = jnp.linalg.cholesky(g_act)
    half_sol = lax.linalg.triangular_solve(factor, rhs, left_side=True, lower=True)
    press = lax.linalg.triangular_solve(
        factor, half_sol, left_side=True, lower=True, transpose_a=True
    )
    return press[:, 0]


def shards(
    disp, stiff, spin, load, foot_node, foot_dest, foot_slot, foot_count, road, active, influence
):
    width_l = disp.shape[2]
    size = road.shape[0]
    kc = stiff[0] - spin[0]
    kl = stiff[1]
    cycle = with_halo(disp, (("circ", 1),), 1, True)
    side = with_halo(disp, (("lat", 2),), 1, False)
    u_next = cycle[:, 2:, :]
    u_prev = cycle[:, :-2, :]
    u_right = side[:, :, 2:]
    u_left = side[:, :, :-2]
    stiff_force = (
        kc * (2.0 * disp - u_next - u_prev) + kl * (2.0 * disp - u_right - u_left) + 0.5 * disp
    )
    resid = load - stiff_force
    diag_k = 2.0 * kc + 2.0 * kl + 0.5
    trial = disp + resid / diag_k
    row_count = foot_node.shape[0]
    live = jnp.arange(row_count, dtype=jnp.int32) < foot_count[0]
    circ_i = foot_node // width_l
    lat_i = foot_node % width_l
    w_rows = trial[2][circ_i, lat_i]
    k_rows = diag_k[circ_i, lat_i]
    owners = lax.axis_size("circ") * lax.axis_size("lat")
    pick = jnp.where(live, foot_dest * size + foot_slot, 0)
    live_f = live.astype(jnp.float32)
    target = jnp.where(live, foot_dest * size + foot_slot, owners * size)
    values = jnp.stack([w_rows, k_rows])
    outgoing = jnp.zeros((2, owners * size), jnp.float32).at[:, target].add(values, mode="drop")
    incoming = lax.all_to_all(
        outgoing.reshape(2, owners, size), ("circ", "lat"), split_axis=1, concat_axis=1, tiled=True
    )
    patch_w = jnp.sum(incoming[0], axis=0)
    patch_k = jnp.sum(incoming[1], axis=0)
    press = solve_patch(patch_w, patch_k, road, active, influence[0])
    senders = incoming[1] > 0.0
    returned = jnp.where(senders, press[None, :], 0.0)
    answers = lax.all_to_all(returned, ("circ", "lat"), split_axis=0, concat_axis=0, tiled=True)
    p_rows = answers.reshape(-1)[pick] * live_f
    contact_force = jnp.zeros(diag_k.shape, jnp.float32).at[circ_i, lat_i].add(p_rows)
    new_disp = trial.at[2].add(-contact_force / diag_k)
    return (new_disp, press)


def solution(mesh):
    return jax.shard_map(
        shards,
        mesh=mesh,
        in_specs=(
            P(None, ("cases", "circ"), "lat"),
            P(None, ("cases", "circ"), "lat"),
            P("cases"),
            P(None, ("cases", "circ"), "lat"),
            P(("cases", "circ", "lat")),
            P(("cases", "circ", "lat")),
            P(("cases", "circ", "lat")),
            P(("cases", "circ", "lat")),
            P(("cases", "circ", "lat")),
            P(("cases", "circ", "lat")),
            P(("cases", "circ", "lat"), None, None),
        ),
        out_specs=(P(None, ("cases", "circ"), "lat"), P(("cases", "circ", "lat"))),
        check_vma=False,
    )
```

profile of v0, /device:TPU:0, one launch (start us, length us, event | category | flops | bytes accessed | tf_op | source)
XLA Modules:
  0.0 218.2 jit_solution(11293435970632719612)
XLA Ops:
  0.7 1.2 fusion.84
  1.8 4.9 %collective-permute-start.3 = (f32[3,128,1]{2,1,0:T(8,128)S(1)}, f32[3,128,1]{2,1,0:T(8,128)S(1)}, u32[]{:S(2)}, u32[]{:S(2)}) collective-permute-start(f32[3,128,1]{2,1,0:T(8,128)S(1)} %get-tuple-element.51), channel_id=1, source_target_pairs={{0,1},{1,2},{2,3},{4,5},{5,6},{6,7},{8,9},{9,10},{10,11},{12,13},{... | collective-permute-start | bytes 4616 | tf_op jit(solution)/shard_map/ppermute | solution.py:15
  6.8 1.3 collective-permute-start.2
  8.1 0.7 fusion.83
  8.8 1.7 collective-permute-start
  11.2 0.9 slice_bitcast_fusion.13
  12.1 0.9 multiply_add_fusion
  13.0 0.7 compare_select_fusion.3
  14.3 0.7 fusion.54
  15.1 6.8 %gather_fusion.1 = f32[1024]{0:T(1024)S(1)} fusion(f32[128,128]{1,0:T(8,128)S(1)} %get-tuple-element.44, s32[1024]{0:T(1024)S(1)} %bitcast.183), kind=kCustom, calls=%fused_computation.1 | custom fusion | bytes 16384 | tf_op jit(solution)/shard_map/gather | solution.py:63
  22.2 6.8 %gather_fusion = f32[1024]{0:T(1024)S(1)} fusion(f32[128,128]{1,0:T(8,128)S(1)} %slice_bitcast_fusion.12, s32[1024]{0:T(1024)S(1)} %bitcast.184), kind=kCustom, calls=%fused_computation | custom fusion | bytes 16384 | tf_op jit(solution)/shard_map/gather | solution.py:62
  29.3 8.2 %scatter_custom_fusion = f32[2,8192]{0,1:T(8,128)} fusion(s32[1024]{0:T(1024)S(1)} %get-tuple-element.62, f32[1024,2]{1,0:T(8,128)S(1)} %copy.35, f32[]{:T(128)} %constant.210.clone.1), kind=kCustom, calls=%fused_computation.7 | custom fusion | flops 2048 | bytes 65540 | tf_op jit(solution)/shard_map/scatter-add | solution.py:69
  37.5 3.5 %copy.36 = f32[2,16,512]{2,0,1:T(2,128)} copy(f32[2,16,512]{0,2,1:T(8,128)} %bitcast.185) | data formatting | bytes 131072 | tf_op jit(solution)/shard_map/reshape | solution.py:71
  40.9 7.2 %all-to-all-start = ((f32[2,16,512]{2,0,1:T(2,128)}), f32[2,16,512]{2,0,1:T(2,128)S(1)}, u32[]{:S(2)}, u32[]{:S(2)}) async-start(f32[2,16,512]{2,0,1:T(2,128)} %copy.36), calls=%async_computation | async-start | bytes 131072 | tf_op jit(solution)/shard_map/all_to_all | solution.py:70
  48.6 5.9 %all-to-all-done = f32[2,16,512]{2,0,1:T(2,128)S(1)} async-done(((f32[2,16,512]{2,0,1:T(2,128)}), f32[2,16,512]{2,0,1:T(2,128)S(1)}, u32[]{:S(2)}, u32[]{:S(2)}) %all-to-all-start) | async-done | bytes 65568 | tf_op jit(solution)/shard_map/all_to_all | solution.py:70
  55.4 11.7 %cholesky.102 = f32[128,128]{1,0:T(8,128)S(1)} custom-call(f32[128,128]{1,0:T(8,128)S(1)} %cholesky.260), custom_call_target="Cholesky" | custom-call | tf_op jit(solution)/shard_map/jit(cholesky)/cholesky | solution.py:31
  67.3 9.8 %custom-call.32 = f32[1,128,128]{1,2,0:T(8,128)S(1)} custom-call(f32[1,128,128]{2,1,0:T(8,128)S(1)} %get-tuple-element.59), custom_call_target="InvertDiagBlocksLowerTriangular" | custom-call | tf_op jit(solution)/shard_map/jit(cholesky)/cholesky | solution.py:31
  77.9 11.7 %cholesky.212 = f32[128,128]{1,0:T(8,128)S(1)} custom-call(f32[128,128]{1,0:T(8,128)S(1)} %cholesky.264), custom_call_target="Cholesky" | custom-call | tf_op jit(solution)/shard_map/jit(cholesky)/cholesky | solution.py:31
  89.9 10.0 %custom-call.33 = f32[1,128,128]{1,2,0:T(8,128)S(1)} custom-call(f32[1,128,128]{2,1,0:T(8,128)S(1)} %get-tuple-element.57), custom_call_target="InvertDiagBlocksLowerTriangular" | custom-call | tf_op jit(solution)/shard_map/jit(cholesky)/cholesky | solution.py:31
  100.9 11.7 %cholesky.233 = f32[128,128]{1,0:T(8,128)S(1)} custom-call(f32[128,128]{1,0:T(8,128)S(1)} %cholesky.269), custom_call_target="Cholesky" | custom-call | tf_op jit(solution)/shard_map/jit(cholesky)/cholesky | solution.py:31
  112.7 9.8 %custom-call.34 = f32[1,128,128]{1,2,0:T(8,128)S(1)} custom-call(f32[1,128,128]{2,1,0:T(8,128)S(1)} %get-tuple-element.55), custom_call_target="InvertDiagBlocksLowerTriangular" | custom-call | tf_op jit(solution)/shard_map/jit(cholesky)/cholesky | solution.py:31
  123.3 12.0 %cholesky.250 = f32[128,128]{1,0:T(8,128)S(1)} custom-call(f32[128,128]{1,0:T(8,128)S(1)} %convolution_subtract_fusion.2), custom_call_target="Cholesky" | custom-call | tf_op jit(solution)/shard_map/jit(cholesky)/cholesky | solution.py:31
  140.7 11.0 %while.2 = (s32[]{:T(128)}, f32[512,512]{0,1:T(8,128)S(1)}, s32[4,2]{0,1:T(2,128)S(1)}, f32[4,128,128]{2,1,0:T(8,128)}, s32[]{:T(128)}) while((s32[]{:T(128)}, f32[512,512]{0,1:T(8,128)S(1)}, s32[4,2]{0,1:T(2,128)S(1)}, f32[4,128,128]{2,1,0:T(8,128)}, s32[]{:T(128)}) %tuple.43), condition=%wide.while_cond.1, body=%wide.while_body.1.sunk | while | flops 2 | bytes 393329 | solution.py:33
  141.3 1.4 dynamic-slice.15
  144.1 1.4 dynamic-slice.15
  146.8 1.4 dynamic-slice.15
  149.5 1.4 dynamic-slice.15
  151.6 40.1 %custom-call.35 = f32[4,128,128]{1,2,0:T(8,128)S(1)} custom-call(f32[4,128,128]{2,1,0:T(8,128)} %get-tuple-element.21), custom_call_target="InvertDiagBlocksLowerTriangular" | custom-call | tf_op jit(solution)/shard_map/triangular_solve | solution.py:33
  195.4 3.5 %all-to-all-start.1 = ((f32[16,1,512]{2,1,0:T(1,128)}), f32[16,1,512]{2,1,0:T(1,128)S(1)}, u32[]{:S(2)}, u32[]{:S(2)}) async-start(f32[16,1,512]{2,1,0:T(1,128)} %copy.48), calls=%async_computation.1 | async-start | bytes 65536 | tf_op jit(solution)/shard_map/all_to_all | solution.py:78
  198.9 6.4 %all-to-all-done.1 = f32[16,1,512]{2,1,0:T(1,128)S(1)} async-done(((f32[16,1,512]{2,1,0:T(1,128)}), f32[16,1,512]{2,1,0:T(1,128)S(1)}, u32[]{:S(2)}, u32[]{:S(2)}) %all-to-all-start.1) | async-done | bytes 32800 | tf_op jit(solution)/shard_map/all_to_all | solution.py:78
  205.3 6.1 %gather_fusion.2 = f32[1024]{0:T(1024)S(1)} fusion(f32[8192]{0:T(1024)S(1)} %bitcast.182, s32[1024]{0:T(1024)S(1)} %get-tuple-element.61), kind=kCustom, calls=%fused_computation.2 | custom fusion | bytes 12288 | tf_op jit(solution)/shard_map/gather | solution.py:79
  211.5 5.9 %scatter_custom_fusion.1 = f32[16384]{0:T(1024)S(1)} fusion(s32[1024]{0:T(1024)S(1)} %broadcast_select_fusion, f32[1024]{0:T(1024)S(1)} %fusion.55, f32[]{:T(128)} %constant.210.clone.1), kind=kCustom, calls=%fused_computation.104 | custom fusion | flops 1024 | bytes 65540
  (102 shorter events, 17.5 us)
Async XLA Ops:
  0.6 21.3 %copy-start = (f32[3,128,128]{2,1,0:T(8,128)S(1)}, f32[3,128,128]{2,1,0:T(8,128)}, u32[]{:S(2)}) copy-start(f32[3,128,128]{2,1,0:T(8,128)} %param.13) | copy-start | bytes 589828
  0.6 21.3 %copy-start.3 = (f32[3,128,128]{2,1,0:T(8,128)S(1)}, f32[3,128,128]{2,1,0:T(8,128)}, u32[]{:S(2)}) copy-start(f32[3,128,128]{2,1,0:T(8,128)} %param.16) | copy-start | bytes 589828
  1.8 20.1 %collective-permute-start.3 = (f32[3,128,1]{2,1,0:T(8,128)S(1)}, f32[3,128,1]{2,1,0:T(8,128)S(1)}, u32[]{:S(2)}, u32[]{:S(2)}) collective-permute-start(f32[3,128,1]{2,1,0:T(8,128)S(1)} %get-tuple-element.51), channel_id=1, source_target_pairs={{0,1},{1,2},{2,3},{4,5},{5,6},{6,7},{8,9},{9,10},{10,11},{12,13},{... | collective-permute-start | bytes 4616 | tf_op jit(solution)/shard_map/ppermute | solution.py:15
  6.8 15.1 %collective-permute-start.2 = (f32[3,128,1]{2,1,0:T(8,128)S(1)}, f32[3,128,1]{2,1,0:T(8,128)S(1)}, u32[]{:S(2)}, u32[]{:S(2)}) collective-permute-start(f32[3,128,1]{2,1,0:T(8,128)S(1)} %get-tuple-element.50), channel_id=1, source_target_pairs={{1,0},{2,1},{3,2},{5,4},{6,5},{7,6},{9,8},{10,9},{11,10},{13,12},{... | collective-permute-start | bytes 4616 | tf_op jit(solution)/shard_map/ppermute | solution.py:17
  8.8 13.1 %collective-permute-start.1 = (f32[3,1,128]{2,1,0:T(1,128)S(1)}, f32[3,1,128]{2,1,0:T(1,128)S(1)}, u32[]{:S(2)}, u32[]{:S(2)}) collective-permute-start(f32[3,1,128]{2,1,0:T(1,128)S(1)} %get-tuple-element.49), channel_id=1, source_target_pairs={{0,4},{4,8},{8,12},{12,0},{1,5},{5,9},{9,13},{13,1},{2,6},{6,10},{... | collective-permute-start | bytes 4616 | tf_op jit(solution)/shard_map/ppermute | solution.py:15
  8.8 13.1 %collective-permute-start = (f32[3,1,128]{2,1,0:T(1,128)S(1)}, f32[3,1,128]{2,1,0:T(1,128)S(1)}, u32[]{:S(2)}, u32[]{:S(2)}) collective-permute-start(f32[3,1,128]{2,1,0:T(1,128)S(1)} %get-tuple-element.48), channel_id=1, source_target_pairs={{4,0},{8,4},{12,8},{0,12},{5,1},{9,5},{13,9},{1,13},{6,2},{10,6},{... | collective-permute-start | bytes 4616 | tf_op jit(solution)/shard_map/ppermute | solution.py:17
  29.3 18.9 %copy-start.1 = (f32[1,512,512]{2,1,0:T(8,128)S(1)}, f32[1,512,512]{2,1,0:T(8,128)}, u32[]{:S(2)}) copy-start(f32[1,512,512]{2,1,0:T(8,128)} %param.23) | copy-start | bytes 3145732
  37.4 11.0 %copy-start.4 = (s32[512]{0:T(512)S(1)}, s32[512]{0:T(512)}, u32[]{:S(2)}) copy-start(s32[512]{0:T(512)} %param.22) | copy-start | bytes 6148
  37.4 11.1 %copy-start.7 = (s32[2]{0:T(128)S(1)}, s32[2]{0:T(128)}, u32[]{:S(2)}) copy-start(s32[2]{0:T(128)} %constant.230) | copy-start | bytes 28
  37.5 17.2 %copy-start.6 = (f32[512]{0:T(512)S(1)}, f32[512]{0:T(512)}, u32[]{:S(2)}) copy-start(f32[512]{0:T(512)} %param.21) | copy-start | bytes 6148
  40.9 13.6 %all-to-all-start = ((f32[2,16,512]{2,0,1:T(2,128)}), f32[2,16,512]{2,0,1:T(2,128)S(1)}, u32[]{:S(2)}, u32[]{:S(2)}) async-start(f32[2,16,512]{2,0,1:T(2,128)} %copy.36), calls=%async_computation | async-start | bytes 131072 | tf_op jit(solution)/shard_map/all_to_all | solution.py:70
  194.7 22.8 %copy-start.5 = (f32[512,1]{0,1:T(1,128)}, f32[512,1]{0,1:T(1,128)S(1)}, u32[]{:S(2)}) copy-start(f32[512,1]{0,1:T(1,128)S(1)} %pad_maximum_fusion.4) | copy-start | bytes 6148
  195.4 9.9 %all-to-all-start.1 = ((f32[16,1,512]{2,1,0:T(1,128)}), f32[16,1,512]{2,1,0:T(1,128)S(1)}, u32[]{:S(2)}, u32[]{:S(2)}) async-start(f32[16,1,512]{2,1,0:T(1,128)} %copy.48), calls=%async_computation.1 | async-start | bytes 65536 | tf_op jit(solution)/shard_map/all_to_all | solution.py:78
  217.5 0.7 copy-start.2
where the time goes:
time: 219 us; the launch traced here: 218 us
  other arithmetic  138 us (63%)
  local copies, waits for them, and re-layouts  39 us (18%)
  starting transfers between devices  18.6 us (8%)
  waiting for transfers between devices  12.4 us (6%)
  matrix products  5.24 us (2%)
  between operations  4.92 us (2%)
    another operation x15, other arithmetic, solve_patch(): factor = jnp.linalg.cholesky(g_act)  79.4 us
    another operation x4, other arithmetic, solve_patch(): lax.linalg.triangular_solve(factor, half_sol, left_side=True, lower=True,...  40.3 us
    another operation x20, local copies, waits for them, and re-layouts  10.9 us
    scatter-add x1, other arithmetic, shards(): jnp.zeros((2, owners * size), jnp.float32).at[:, target]  8.16 us
    all_to_all x1, starting transfers between devices, shards(): lax.all_to_all(outgoing.reshape(2, owners, size), ('circ', 'lat'), split_...  7.16 us
    gather x1, local copies, waits for them, and re-layouts, shards(): k_rows = diag_k[circ_i, lat_i]  6.8 us
    gather x1, local copies, waits for them, and re-layouts, shards(): w_rows = trial[2][circ_i, lat_i]  6.8 us
    all_to_all x1, waiting for transfers between devices, shards(): lax.all_to_all(returned, ('circ', 'lat'), split_axis=0, concat_axis=0, ti...  6.43 us
  transfers between devices with their start and end apart: 6, of which 2 were waited for; matrix products, arithmetic and copies ran while one was open for 5% of the time, Pallas kernels for 0%

commit v1 on v0

v1 whole, which is shorter than its diff:
```python
import functools

import jax
import jax.numpy as jnp
from jax import lax
from jax.experimental import pallas as pl
from jax.experimental.pallas import tpu as pltpu
from jax.sharding import PartitionSpec as P

F32 = jnp.float32
BF16 = jnp.bfloat16
I32 = jnp.int32
LANES = 128
CG_STEPS = 40
CG_STOP = 1e-13
TRUE_STOP = 1e-12


def log2(value):
    assert value > 0 and value & (value - 1) == 0
    return value.bit_length() - 1


def thirds(x):
    high = x.astype(BF16).astype(F32)
    rest = x - high
    mid = rest.astype(BF16).astype(F32)
    return high, mid, rest - mid


def iota(shape, axis):
    return lax.broadcasted_iota(I32, shape, axis)


def wide(ref, first, count):
    return jnp.concatenate([ref[i : i + 1, :] for i in range(first, first + count)], axis=1)


def shifted(u):
    rows, cols = u.shape
    row, col = iota(u.shape, 0), iota(u.shape, 1)
    return (
        jnp.where(row == rows - 1, 0.0, pltpu.roll(u, rows - 1, 0)),
        jnp.where(row == 0, 0.0, pltpu.roll(u, 1, 0)),
        jnp.where(col == cols - 1, 0.0, pltpu.roll(u, cols - 1, 1)),
        jnp.where(col == 0, 0.0, pltpu.roll(u, 1, 1)),
    )


def edges(u):
    rows, cols = u.shape
    turned = u.T
    return [u[0:1, :], u[rows - 1 : rows, :], turned[0:1, :], turned[cols - 1 : cols, :]]


def pack_kernel(count, spin, disp, stiff, load, node, dest, slot, send, late):
    owners = send.shape[0]
    rows, cols = disp.shape[1:]
    chunks = node.shape[0]
    size = 4 * LANES
    kc = stiff[0] - spin[0]
    kl = stiff[1]
    u = disp[2]
    u_next, u_prev, u_right, u_left = shifted(u)
    force = kc * (2.0 * u - u_next - u_prev) + kl * (2.0 * u - u_right - u_left) + 0.5 * u
    inner = u + (load[2] - force) / (2.0 * kc + 2.0 * kl + 0.5)
    table = jnp.concatenate(
        [jnp.concatenate(thirds(x), axis=1) for x in (inner, kc, kl)], axis=0
    ).astype(BF16)
    step = 2 if chunks % 2 == 0 else 1
    span = step * LANES
    left, right = [], []
    for first in range(0, chunks, step):
        nodes = wide(node, first, step)
        owner = wide(dest, first, step)
        live = iota((1, span), 1) + first * LANES < count[0]
        owner = jnp.where(live, owner, -1)
        circ = nodes >> log2(cols)
        lat = nodes & (cols - 1)
        one_lat = (iota((cols, span), 0) == lat).astype(BF16)
        picked = jnp.dot(
            table, jnp.concatenate([one_lat] * 3, axis=0), preferred_element_type=F32
        )
        one_circ = iota((rows, span), 0) == circ
        pieces = []
        for k in range(3):
            block = picked[k * rows : (k + 1) * rows]
            pieces += thirds(jnp.sum(jnp.where(one_circ, block, 0.0), axis=0, keepdims=True))
        pieces += [(circ * cols).astype(F32), lat.astype(F32)]
        to = iota((owners, span), 0) == owner
        left.append(
            jnp.concatenate([jnp.where(to, x, 0.0) for x in pieces], axis=0).astype(BF16)
        )
        right.append((iota((size, span), 0) == wide(slot, first, step)).astype(BF16))
    spread = lax.dot_general(
        jnp.concatenate(left, axis=1),
        jnp.concatenate(right, axis=1),
        (((1,), (1,)), ((), ())),
        preferred_element_type=F32,
    )
    part = [spread[i * owners : (i + 1) * owners] for i in range(11)]
    values = [sum(part[3 * k + 1 : 3 * k + 3], part[3 * k]) for k in range(3)] + [part[9] + part[10]]
    for v in range(4):
        for j in range(4):
            send[:, 4 * v + j, :] = values[v][:, j * LANES : (j + 1) * LANES]
    for t, edge in enumerate(edges(u) + edges(disp[0])):
        send[:, 16 + t, :] = jnp.broadcast_to(edge, (owners, LANES))
    for t, edge in enumerate(edges(disp[1])):
        late[t : t + 1, :] = edge


def column(row):
    return jnp.broadcast_to(row, (LANES, row.shape[1])).T


def patch_system(lats, got, road, active):
    owners = got.shape[0]
    rows = cols = LANES
    size = 4 * LANES
    total = jnp.sum(got[:, 0:16, :], axis=0)
    here = got[:, 4:8, :] > 0.0
    sender = jnp.sum(jnp.where(here, lax.broadcasted_iota(I32, here.shape, 0), 0), axis=0)
    w, kc, kl, node = [wide(total, 4 * v, 4) for v in range(4)]
    node = node.astype(I32)
    sender = wide(sender, 0, 4)
    circ = node >> log2(cols)
    lat = node & (cols - 1)
    after = sender + lats
    after = jnp.where(after >= owners, after - owners, after)
    before = sender - lats
    before = jnp.where(before < 0, before + owners, before)
    side = sender & (lats - 1)
    from_circ = jnp.where(
        circ == rows - 1, after * 8, jnp.where(circ == 0, before * 8 + 1, -1)
    )
    from_lat = jnp.where(
        (lat == cols - 1) & (side < lats - 1),
        sender * 8 + 10,
        jnp.where((lat == 0) & (side > 0), sender * 8 - 5, -1),
    )
    layers = got[:, 16:24, :].reshape(owners * 8, LANES)
    layers = jnp.concatenate(thirds(layers), axis=1).astype(BF16)

    def pick(high, low):
        one = (iota((LANES, size), 0) == low).astype(BF16)
        found = jnp.dot(layers, jnp.concatenate([one] * 3, axis=0), preferred_element_type=F32)
        return jnp.sum(
            jnp.where(iota((owners * 8, size), 0) == high, found, 0.0), axis=0, keepdims=True
        )

    diag_k = 2.0 * kc + 2.0 * kl + 0.5
    w = w + (kc * pick(from_circ, lat) + kl * pick(from_lat, circ)) / diag_k
    mask = wide(active, 0, 4).astype(F32)
    return mask, mask * (w - wide(road, 0, 4)), 1.0 / diag_k


def factor_solve(block, mask, rhs, soft, work, press):
    size = rhs.shape[1]
    row = iota((size, 1), 0)
    lane = iota((1, LANES), 1)
    down = column(mask)
    for t in range(size // LANES):
        part = slice(t * LANES, (t + 1) * LANES)
        on = row == lane + t * LANES
        live = mask[:, part]
        work[:, part] = down * live * (block[:, part] + jnp.where(on, soft[:, part], 0.0)) + (
            jnp.where(on, 1.0 - live, 0.0)
        )
    work[:, size:] = column(rhs)
    place = iota((1, size), 1)

    def eliminate(j, carry):
        pivot_row = work[pl.ds(j, 1), :]
        pivot = jnp.sum(jnp.where(place == j, pivot_row[:, :size], 0.0), axis=1, keepdims=True)
        start = pl.multiple_of((j >> log2(LANES)) << log2(LANES), LANES)
        tile = work[:, pl.ds(start, LANES)]
        below = jnp.sum(jnp.where(lane == j - start, tile, 0.0), axis=1, keepdims=True)
        ratio = jnp.where(row > j, below / pivot, 0.0)
        work[...] = work[...] - ratio * pivot_row
        return carry

    lax.fori_loop(0, size, eliminate, 0)

    def substitute(step, x):
        j = size - 1 - step
        now = work[pl.ds(j, 1), :]
        upper = now[:, :size]
        pivot = jnp.sum(jnp.where(place == j, upper, 0.0), axis=1, keepdims=True)
        known = jnp.sum(upper * x, axis=1, keepdims=True)
        return jnp.where(place == j, (now[:, size : size + 1] - known) / pivot, x)

    press[...] = lax.fori_loop(0, size, substitute, jnp.zeros((1, size), F32))


def over(top, bottom):
    return jnp.where(bottom > 0.0, top / bottom, 0.0)


def dot(a, b):
    return jnp.sum(a * b, axis=1, keepdims=True)


def solve_kernel(lats, got, road, active, late, block, send, pressure, work, press):
    size = 4 * LANES
    mask, rhs, soft = patch_system(lats, got, road, active)
    factor_solve(block, mask, rhs, soft, work, press)
    answer = press[...]
    for j in range(4):
        part = answer[:, j * LANES : (j + 1) * LANES]
        pressure[j : j + 1, :] = part
        send[:, j, :] = jnp.broadcast_to(part, (send.shape[0], LANES))
        send[:, 4 + j, :] = jnp.broadcast_to(late[j : j + 1, :], (send.shape[0], LANES))


def finish_kernel(
    axes, count, spin, disp, stiff, load, node, dest, slot, got, back, out
):
    circs, lats = axes
    owners = got.shape[0]
    rows, cols = disp.shape[1:]
    chunks = node.shape[0]
    size = 4 * LANES
    my_circ, my_lat = lax.axis_index("circ"), lax.axis_index("lat")
    me = my_circ * lats + my_lat
    after = jnp.where(my_circ == circs - 1, my_lat, me + lats)
    before = jnp.where(my_circ == 0, (circs - 1) * lats + my_lat, me - lats)
    right_dev = jnp.minimum(me + 1, owners - 1)
    left_dev = jnp.maximum(me - 1, 0)
    kc = stiff[0] - spin[0]
    kl = stiff[1]
    diag_k = 2.0 * kc + 2.0 * kl + 0.5
    row, col = iota((rows, cols), 0), iota((rows, cols), 1)
    trial = []
    for c in range(3):
        u = disp[c]
        source, base = ((got, 20), (back, 4), (got, 16))[c]
        u_next, u_prev, u_right, u_left = shifted(u)
        u_next = jnp.where(row == rows - 1, source[after, base : base + 1, :], u_next)
        u_prev = jnp.where(row == 0, source[before, base + 1 : base + 2, :], u_prev)
        from_right = jnp.where(my_lat < lats - 1, source[right_dev, base + 2 : base + 3, :], 0.0)
        from_left = jnp.where(my_lat > 0, source[left_dev, base + 3 : base + 4, :], 0.0)
        u_right = jnp.where(col == cols - 1, column(from_right), u_right)
        u_left = jnp.where(col == 0, column(from_left), u_left)
        force = kc * (2.0 * u - u_next - u_prev) + kl * (2.0 * u - u_right - u_left) + 0.5 * u
        trial.append(u + (load[c] - force) / diag_k)
    out[0] = trial[0]
    out[1] = trial[1]

    answers = jnp.concatenate([back[:, j, :] for j in range(4)], axis=1)
    answers = jnp.concatenate(thirds(answers), axis=0).astype(BF16)
    step = 2 if chunks % 2 == 0 else 1
    span = step * LANES
    left, right = [], []
    for first in range(0, chunks, step):
        nodes = wide(node, first, step)
        owner = wide(dest, first, step)
        live = iota((1, span), 1) + first * LANES < count[0]
        owner = jnp.where(live, owner, -1)
        circ = nodes >> log2(cols)
        lat = nodes & (cols - 1)
        one_slot = (iota((size, span), 0) == wide(slot, first, step)).astype(BF16)
        found = jnp.dot(answers, one_slot, preferred_element_type=F32)
        found = found[:owners] + found[owners : 2 * owners] + found[2 * owners :]
        push = jnp.sum(
            jnp.where(iota((owners, span), 0) == owner, found, 0.0), axis=0, keepdims=True
        )
        one_circ = iota((rows, span), 0) == circ
        left.append(
            jnp.concatenate(
                [jnp.where(one_circ, x, 0.0) for x in thirds(push)], axis=0
            ).astype(BF16)
        )
        right.append((iota((cols, span), 0) == lat).astype(BF16))
    force = lax.dot_general(
        jnp.concatenate(left, axis=1),
        jnp.concatenate(right, axis=1),
        (((1,), (1,)), ((), ())),
        preferred_element_type=F32,
    )
    force = force[:rows] + force[rows : 2 * rows] + force[2 * rows :]
    out[2] = trial[2] - force / diag_k


def shards(
    disp, stiff, spin, load, foot_node, foot_dest, foot_slot, foot_count, road, active, influence
):
    circs, lats = lax.axis_size("circ"), lax.axis_size("lat")
    owners = circs * lats
    size = road.shape[0]
    rows, cols = disp.shape[1:]
    assert rows == cols == LANES and size == 4 * LANES
    scalar = pl.BlockSpec(memory_space=pltpu.SMEM)
    block = pl.BlockSpec(memory_space=pltpu.VMEM)
    params = pltpu.CompilerParams(vmem_limit_bytes=48 * 1024 * 1024)
    lists = [x.reshape(-1, LANES) for x in (foot_node, foot_dest, foot_slot)]
    send, late = pl.pallas_call(
        pack_kernel,
        in_specs=[scalar, scalar] + [block] * 6,
        out_specs=[block, block],
        out_shape=[
            jax.ShapeDtypeStruct((owners, 24, LANES), F32),
            jax.ShapeDtypeStruct((4, LANES), F32),
        ],
        compiler_params=params,
        name="pack_rows",
    )(foot_count, spin, disp, stiff, load, *lists)
    got = lax.all_to_all(send, ("circ", "lat"), split_axis=0, concat_axis=0, tiled=True)
    reply, pressure = pl.pallas_call(
        functools.partial(solve_kernel, lats),
        in_specs=[block] * 5,
        out_specs=[block, block],
        out_shape=[
            jax.ShapeDtypeStruct((owners, 8, LANES), F32),
            jax.ShapeDtypeStruct((4, LANES), F32),
        ],
        scratch_shapes=[pltpu.VMEM((size, size + LANES), F32), pltpu.VMEM((1, size), F32)],
        compiler_params=params,
        name="solve_patch",
    )(got, road.reshape(4, LANES), active.reshape(4, LANES), late, influence[0])
    back = lax.all_to_all(reply, ("circ", "lat"), split_axis=0, concat_axis=0, tiled=True)
    new_disp = pl.pallas_call(
        functools.partial(finish_kernel, (circs, lats)),
        in_specs=[scalar, scalar] + [block] * 8,
        out_specs=block,
        out_shape=jax.ShapeDtypeStruct(disp.shape, F32),
        compiler_params=params,
        name="finish_nodes",
    )(foot_count, spin, disp, stiff, load, *lists, got, back)
    return (new_disp, pressure.reshape(size))


def solution(mesh):
    return jax.shard_map(
        shards,
        mesh=mesh,
        in_specs=(
            P(None, ("cases", "circ"), "lat"),
            P(None, ("cases", "circ"), "lat"),
            P("cases"),
            P(None, ("cases", "circ"), "lat"),
            P(("cases", "circ", "lat")),
            P(("cases", "circ", "lat")),
            P(("cases", "circ", "lat")),
            P(("cases", "circ", "lat")),
            P(("cases", "circ", "lat")),
            P(("cases", "circ", "lat")),
            P(("cases", "circ", "lat"), None, None),
        ),
        out_specs=(P(None, ("cases", "circ"), "lat"), P(("cases", "circ", "lat"))),
        check_vma=False,
    )
```

time: 219 us -> 240 us (1.096)
  Pallas kernels: 0 us -> 206 us
  other arithmetic: 138 us -> 0 us
  local copies, waits for them, and re-layouts: 39 us -> 5.39 us
  blocking collectives: 0 us -> 25.7 us
  starting transfers between devices: 18.6 us -> 0 us
  waiting for transfers between devices: 12.4 us -> 0 us
  matrix products: 5.24 us -> 0 us
  between operations: 4.92 us -> 2.01 us
    pallas_call x0 -> x3, Pallas kernels: none -> 206 us  [the longest x1 204 us: shards(): pl.pallas_call(functools.partial(solve_kernel, lats), in_specs=[block] *...]
    another operation x20 -> x0, other arithmetic: 120 us -> none  [the longest x15 79.4 us: solve_patch(): factor = jnp.linalg.cholesky(g_act)]
    all_to_all x0 -> x2, blocking collectives: none -> 25.7 us  [the longest x1 15.3 us: shards(): lax.all_to_all(send, ('circ', 'lat'), split_axis=0, concat_axis=0, tiled=...]
    gather x3 -> x0, local copies, waits for them, and re-layouts: 19.7 us -> none  [the longest x1 6.8 us: shards(): k_rows = diag_k[circ_i, lat_i]]
    all_to_all x2 -> x0, waiting for transfers between devices: 12.4 us -> none  [the longest x1 6.43 us: shards(): lax.all_to_all(returned, ('circ', 'lat'), split_axis=0, concat_axis=0, ti...]
    another operation x35 -> x0, local copies, waits for them, and re-layouts: 11.8 us -> none
    all_to_all x2 -> x0, starting transfers between devices: 10.7 us -> none  [the longest x1 7.16 us: shards(): lax.all_to_all(outgoing.reshape(2, owners, size), ('circ', 'lat'), split_...]
    scatter-add x2 -> x0, other arithmetic: 8.19 us -> none  [the longest x1 8.16 us: shards(): jnp.zeros((2, owners * size), jnp.float32).at[:, target]]
  transfers between devices with their start and end apart: 6 -> 0, of which waited for: 2 -> 0; matrix products, arithmetic and copies ran while one was open for 5% -> 0% of each run, Pallas kernels for 0% -> 0%
where the time goes in v1:
time: 240 us
  Pallas kernels  206 us (86%)
  blocking collectives  25.7 us (11%)
  local copies, waits for them, and re-layouts  5.39 us (2%)
    pallas_call x1, Pallas kernels, shards(): pl.pallas_call(functools.partial(solve_kernel, lats), in_specs=[block] *...  204 us
    all_to_all x1, blocking collectives, shards(): lax.all_to_all(send, ('circ', 'lat'), split_axis=0, concat_axis=0, tiled=...  15.3 us
    all_to_all x1, blocking collectives, shards(): lax.all_to_all(reply, ('circ', 'lat'), split_axis=0, concat_axis=0, tiled...  10.4 us
    unnamed x26, local copies, waits for them, and re-layouts  5.39 us

profile of v1, /device:TPU:0, one launch (start us, length us, event | category | flops | bytes accessed | tf_op | source)
XLA Modules:
  0.0 239.6 jit_solution(12998107733229502723)
XLA Ops:
  0.6 0.0 copy-start.8
  1.3 0.0 copy-start.7
  2.0 0.0 copy-done.8
  2.0 0.0 copy-done.7
  2.0 0.0 copy-start.1
  2.0 0.9 copy-done.1
  2.9 0.0 copy-start.3
  2.9 0.9 copy-done.3
  3.8 0.0 copy-start.5
  3.8 0.9 copy-done.5
  4.8 0.0 copy-start.9
  4.8 0.7 copy-done.9
  5.4 1.0 pack_rows.1
  6.5 15.3 %all_to_all.10.got = f32[16,24,128]{2,1,0:T(8,128)S(1)} all-to-all(f32[16,24,128]{2,1,0:T(8,128)S(1)} %get-tuple-element.6), channel_id=1, replica_groups=mesh['cases'=2,'circ'=4,'lat'=4] {'circ','lat'}, dimensions={0} | all-to-all | bytes 393216 | tf_op jit(solution)/shard_map/all_to_all | solution.py:307
  21.8 0.0 copy-start.12
  21.8 0.0 copy-start.11
  21.8 0.7 copy-done.12
  22.5 0.0 copy-done.11
  22.5 0.0 copy-start
  22.5 1.2 copy-done
  23.7 0.0 copy-start.2
  23.7 0.0 copy-start.4
  23.7 0.0 copy-start.10
  23.7 204.1 %solve_patch.1 = (f32[16,8,128]{2,1,0:T(8,128)S(1)}, f32[4,128]{1,0:T(4,128)}) custom-call(f32[16,24,128]{2,1,0:T(8,128)S(1)} %all_to_all.10.got, f32[4,128]{1,0:T(4,128)S(1)} %bitcast.14, s32[4,128]{1,0:T(4,128)S(1)} %bitcast.15, f32[4,128]{1,0:T(4,128)S(1)} %get-tuple-element.7.late, f32[512,512]{1,0:T(8,128)S(1)} %bitcast.7), custom_call_target="tpu_custom_call" | custom-call | tf_op jit(solution)/shard_map/solve_patch/pallas_call | solution.py:308
  227.8 0.0 copy-start.6
  227.8 10.4 %all_to_all.11.back = f32[16,8,128]{2,1,0:T(8,128)S(1)} all-to-all(f32[16,8,128]{2,1,0:T(8,128)S(1)} %get-tuple-element.8), channel_id=1, replica_groups=mesh['cases'=2,'circ'=4,'lat'=4] {'circ','lat'}, dimensions={0} | all-to-all | bytes 131072 | tf_op jit(solution)/shard_map/all_to_all | solution.py:320
  238.2 0.0 copy-done.2
  238.2 0.0 copy-done.4
  238.2 0.0 copy-done.10
  238.2 0.0 copy-done.6
  238.2 1.4 finish_nodes.1
Async XLA Ops:
  0.6 1.3 copy-start.8
  1.3 0.7 copy-start.7
  2.0 0.9 copy-start.1
  2.9 0.9 copy-start.3
  3.8 0.9 copy-start.5
  4.8 0.7 copy-start.9
  21.8 0.7 copy-start.12
  21.8 0.7 copy-start.11
  22.5 1.2 copy-start
  23.7 214.5 %copy-start.2 = (f32[3,128,128]{2,1,0:T(8,128)S(1)}, f32[3,128,128]{2,1,0:T(8,128)}, u32[]{:S(2)}) copy-start(f32[3,128,128]{2,1,0:T(8,128)} %disp.3) | copy-start | bytes 589828
  23.7 214.5 %copy-start.4 = (f32[3,128,128]{2,1,0:T(8,128)S(1)}, f32[3,128,128]{2,1,0:T(8,128)}, u32[]{:S(2)}) copy-start(f32[3,128,128]{2,1,0:T(8,128)} %load.3) | copy-start | bytes 589828
  23.7 214.5 %copy-start.10 = (s32[1024]{0:T(1024)S(1)}, s32[1024]{0:T(1024)}, u32[]{:S(2)}) copy-start(s32[1024]{0:T(1024)} %param.17) | copy-start | bytes 12292
  227.8 10.4 %copy-start.6 = (f32[2,128,128]{2,1,0:T(8,128)S(1)}, f32[2,128,128]{2,1,0:T(8,128)}, u32[]{:S(2)}) copy-start(f32[2,128,128]{2,1,0:T(8,128)} %stiff.3) | copy-start | bytes 393220

commit v2 on v1

--- a/solution.py
+++ b/solution.py
@@ -200,10 +200,58 @@
     return jnp.sum(a * b, axis=1, keepdims=True)
 
 
+def times(block, u, mask, soft):
+    down = column(u)
+    parts = [
+        jnp.sum(block[:, first : first + LANES] * down, axis=0, keepdims=True)
+        for first in range(0, u.shape[1], LANES)
+    ]
+    return mask * (jnp.concatenate(parts, axis=1) + soft * u)
+
+
 def solve_kernel(lats, got, road, active, late, block, send, pressure, work, press):
     size = 4 * LANES
     mask, rhs, soft = patch_system(lats, got, road, active)
-    factor_solve(block, mask, rhs, soft, work, press)
+    square = iota((LANES, LANES), 0) == iota((LANES, LANES), 1)
+    diagonal = jnp.concatenate(
+        [
+            jnp.sum(
+                jnp.where(square, block[i : i + LANES, i : i + LANES], 0.0), axis=0, keepdims=True
+            )
+            for i in range(0, size, LANES)
+        ],
+        axis=1,
+    )
+    scale = mask / (diagonal + soft)
+    start = dot(rhs, scale * rhs)
+
+    def advance(x, r, p, s, norm, alpha):
+        u = scale * r
+        w = times(block, u, mask, soft)
+        now = dot(r, u)
+        beta = over(now, norm)
+        alpha = over(now, dot(w, u) - over(beta * now, alpha))
+        p = u + beta * p
+        s = w + beta * s
+        return x + alpha * p, r - alpha * s, p, s, now, alpha
+
+    def going(state):
+        step, norm = state[0], state[5]
+        return (step < CG_STEPS) & (norm[0, 0] > CG_STOP * start[0, 0])
+
+    def body(state):
+        return (state[0] + 2,) + advance(*advance(*state[1:]))
+
+    zero = jnp.zeros((1, size), F32)
+    none = jnp.zeros((1, 1), F32)
+    x = lax.while_loop(going, body, (0, zero, rhs, zero, zero, start, none))[1]
+    gap = rhs - times(block, x, mask, soft)
+    press[...] = x
+
+    @pl.when(jnp.logical_not(dot(gap, scale * gap)[0, 0] <= TRUE_STOP * start[0, 0]))
+    def _():
+        factor_solve(block, mask, rhs, soft, work, press)
+
     answer = press[...]
     for j in range(4):
         part = answer[:, j * LANES : (j + 1) * LANES]

time: 240 us -> 39.3 us (0.16)
  Pallas kernels: 206 us -> 5.78 us
    pallas_call x1, Pallas kernels: 204 us -> 3.38 us  [shards(): pl.pallas_call(functools.partial(solve_kernel, lats), in_specs=[block] *...]
where the time goes in v2:
time: 39.3 us; the launch traced here: 38.9 us
  blocking collectives  25.7 us (65%)
  Pallas kernels  5.78 us (15%)
  local copies, waits for them, and re-layouts  5.39 us (14%)
  between operations  2.01 us (5%)
    all_to_all x1, blocking collectives, shards(): lax.all_to_all(send, ('circ', 'lat'), split_axis=0, concat_axis=0, tiled=...  15.3 us
    all_to_all x1, blocking collectives, shards(): lax.all_to_all(reply, ('circ', 'lat'), split_axis=0, concat_axis=0, tiled...  10.4 us
    unnamed x26, local copies, waits for them, and re-layouts  5.39 us
    pallas_call x1, Pallas kernels, shards(): pl.pallas_call(functools.partial(solve_kernel, lats), in_specs=[block] *...  3.38 us
    pallas_call x1, Pallas kernels, shards(): pl.pallas_call(functools.partial(finish_kernel, (circs, lats)), in_specs=...  1.36 us
    pallas_call x1, Pallas kernels, shards(): pl.pallas_call(pack_kernel, in_specs=[scalar, scalar] + [block] * 6, out_...  1.05 us

profile of v2, /device:TPU:0, one launch (start us, length us, event | category | flops | bytes accessed | tf_op | source)
XLA Modules:
  0.0 38.9 jit_solution(8209068670397432380)
XLA Ops:
  0.6 0.0 copy-start.8
  1.3 0.0 copy-start.7
  2.0 0.0 copy-done.8
  2.0 0.0 copy-done.7
  2.0 0.0 copy-start.1
  2.0 0.9 %copy-done.1 = f32[3,128,128]{2,1,0:T(8,128)S(1)} copy-done((f32[3,128,128]{2,1,0:T(8,128)S(1)}, f32[3,128,128]{2,1,0:T(8,128)}, u32[]{:S(2)}) %copy-start.1) | copy-done | bytes 196632
  2.9 0.0 copy-start.3
  2.9 0.9 %copy-done.3 = f32[3,128,128]{2,1,0:T(8,128)S(1)} copy-done((f32[3,128,128]{2,1,0:T(8,128)S(1)}, f32[3,128,128]{2,1,0:T(8,128)}, u32[]{:S(2)}) %copy-start.3) | copy-done | bytes 196632
  3.8 0.0 copy-start.5
  3.8 0.9 %copy-done.5 = f32[2,128,128]{2,1,0:T(8,128)S(1)} copy-done((f32[2,128,128]{2,1,0:T(8,128)S(1)}, f32[2,128,128]{2,1,0:T(8,128)}, u32[]{:S(2)}) %copy-start.5) | copy-done | bytes 131096
  4.8 0.0 copy-start.9
  4.8 0.7 %copy-done.9 = s32[1024]{0:T(1024)S(1)} copy-done((s32[1024]{0:T(1024)S(1)}, s32[1024]{0:T(1024)}, u32[]{:S(2)}) %copy-start.9) | copy-done | bytes 4120
  5.4 1.0 %pack_rows.1 = (f32[16,24,128]{2,1,0:T(8,128)S(1)}, f32[4,128]{1,0:T(4,128)S(1)}) custom-call(s32[1]{0:T(128)S(6)} %copy.14.count, f32[1]{0:T(128)S(6)} %copy.13.spin, f32[3,128,128]{2,1,0:T(8,128)S(1)} %copy-done.1, f32[2,128,128]{2,1,0:T(8,128)S(1)} %copy-done.5, f32[3,128,128]{2,1,0:T(8,128)S(1)} %copy-done.3, s32[8,128]{1,0:T(8,128)S(1)} %bitcast.8, ...), custom_call_target="tpu_custom_call" | custom-call | tf_op jit(solution)/shard_map/pack_rows/pallas_call | solution.py:344
  6.5 15.3 %all_to_all.10.got = f32[16,24,128]{2,1,0:T(8,128)S(1)} all-to-all(f32[16,24,128]{2,1,0:T(8,128)S(1)} %get-tuple-element.6), channel_id=1, replica_groups=mesh['cases'=2,'circ'=4,'lat'=4] {'circ','lat'}, dimensions={0} | all-to-all | bytes 393216 | tf_op jit(solution)/shard_map/all_to_all | solution.py:355
  21.8 0.0 copy-start.12
  21.8 0.0 copy-start.11
  21.8 0.7 %copy-done.12 = s32[512]{0:T(512)S(1)} copy-done((s32[512]{0:T(512)S(1)}, s32[512]{0:T(512)}, u32[]{:S(2)}) %copy-start.12) | copy-done | bytes 2072
  22.5 0.0 copy-done.11
  22.5 0.0 copy-start
  22.5 1.2 %copy-done = f32[1,512,512]{2,1,0:T(8,128)S(1)} copy-done((f32[1,512,512]{2,1,0:T(8,128)S(1)}, f32[1,512,512]{2,1,0:T(8,128)}, u32[]{:S(2)}) %copy-start) | copy-done | bytes 1048600
  23.7 0.0 copy-start.2
  23.7 0.0 copy-start.4
  23.7 0.0 copy-start.10
  23.7 3.4 %solve_patch.1 = (f32[16,8,128]{2,1,0:T(8,128)S(1)}, f32[4,128]{1,0:T(4,128)}) custom-call(f32[16,24,128]{2,1,0:T(8,128)S(1)} %all_to_all.10.got, f32[4,128]{1,0:T(4,128)S(1)} %bitcast.14, s32[4,128]{1,0:T(4,128)S(1)} %bitcast.15, f32[4,128]{1,0:T(4,128)S(1)} %get-tuple-element.7.late, f32[512,512]{1,0:T(8,128)S(1)} %bitcast.7), custom_call_target="tpu_custom_call" | custom-call | tf_op jit(solution)/shard_map/solve_patch/pallas_call | solution.py:356
  27.1 0.0 copy-start.6
  27.1 10.4 %all_to_all.11.back = f32[16,8,128]{2,1,0:T(8,128)S(1)} all-to-all(f32[16,8,128]{2,1,0:T(8,128)S(1)} %get-tuple-element.8), channel_id=1, replica_groups=mesh['cases'=2,'circ'=4,'lat'=4] {'circ','lat'}, dimensions={0} | all-to-all | bytes 131072 | tf_op jit(solution)/shard_map/all_to_all | solution.py:368
  37.5 0.0 copy-done.2
  37.5 0.0 copy-done.4
  37.5 0.0 copy-done.10
  37.5 0.0 copy-done.6
  37.5 1.4 %finish_nodes.1 = f32[3,128,128]{2,1,0:T(8,128)} custom-call(s32[1]{0:T(128)S(6)} %copy.14.count, f32[1]{0:T(128)S(6)} %copy.13.spin, f32[3,128,128]{2,1,0:T(8,128)S(1)} %copy-done.2, f32[2,128,128]{2,1,0:T(8,128)S(1)} %copy-done.6, f32[3,128,128]{2,1,0:T(8,128)S(1)} %copy-done.4, s32[8,128]{1,0:T(8,128)S(1)} %bitcast.9, s32[8,128]{1,0:T(8,128)S(1)} %bitcast.11, ...), custom_call_target="tpu_custom_call" | custom-call | tf_op jit(solution)/shard_map/finish_nodes/pallas_call | solution.py:369
Async XLA Ops:
  0.6 1.3 %copy-start.8 = (s32[1024]{0:T(1024)S(1)}, s32[1024]{0:T(1024)}, u32[]{:S(2)}) copy-start(s32[1024]{0:T(1024)} %param.16) | copy-start | bytes 12292
  1.3 0.7 %copy-start.7 = (s32[1024]{0:T(1024)S(1)}, s32[1024]{0:T(1024)}, u32[]{:S(2)}) copy-start(s32[1024]{0:T(1024)} %param.15) | copy-start | bytes 12292
  2.0 0.9 %copy-start.1 = (f32[3,128,128]{2,1,0:T(8,128)S(1)}, f32[3,128,128]{2,1,0:T(8,128)}, u32[]{:S(2)}) copy-start(f32[3,128,128]{2,1,0:T(8,128)} %disp.3) | copy-start | bytes 589828
  2.9 0.9 %copy-start.3 = (f32[3,128,128]{2,1,0:T(8,128)S(1)}, f32[3,128,128]{2,1,0:T(8,128)}, u32[]{:S(2)}) copy-start(f32[3,128,128]{2,1,0:T(8,128)} %load.3) | copy-start | bytes 589828
  3.8 0.9 %copy-start.5 = (f32[2,128,128]{2,1,0:T(8,128)S(1)}, f32[2,128,128]{2,1,0:T(8,128)}, u32[]{:S(2)}) copy-start(f32[2,128,128]{2,1,0:T(8,128)} %stiff.3) | copy-start | bytes 393220
  4.8 0.7 %copy-start.9 = (s32[1024]{0:T(1024)S(1)}, s32[1024]{0:T(1024)}, u32[]{:S(2)}) copy-start(s32[1024]{0:T(1024)} %param.17) | copy-start | bytes 12292
  21.8 0.7 %copy-start.12 = (s32[512]{0:T(512)S(1)}, s32[512]{0:T(512)}, u32[]{:S(2)}) copy-start(s32[512]{0:T(512)} %param.20) | copy-start | bytes 6148
  21.8 0.7 %copy-start.11 = (f32[512]{0:T(512)S(1)}, f32[512]{0:T(512)}, u32[]{:S(2)}) copy-start(f32[512]{0:T(512)} %param.19) | copy-start | bytes 6148
  22.5 1.2 %copy-start = (f32[1,512,512]{2,1,0:T(8,128)S(1)}, f32[1,512,512]{2,1,0:T(8,128)}, u32[]{:S(2)}) copy-start(f32[1,512,512]{2,1,0:T(8,128)} %param.21) | copy-start | bytes 3145732
  23.7 13.8 %copy-start.2 = (f32[3,128,128]{2,1,0:T(8,128)S(1)}, f32[3,128,128]{2,1,0:T(8,128)}, u32[]{:S(2)}) copy-start(f32[3,128,128]{2,1,0:T(8,128)} %disp.3) | copy-start | bytes 589828
  23.7 13.8 %copy-start.4 = (f32[3,128,128]{2,1,0:T(8,128)S(1)}, f32[3,128,128]{2,1,0:T(8,128)}, u32[]{:S(2)}) copy-start(f32[3,128,128]{2,1,0:T(8,128)} %load.3) | copy-start | bytes 589828
  23.7 13.8 %copy-start.10 = (s32[1024]{0:T(1024)S(1)}, s32[1024]{0:T(1024)}, u32[]{:S(2)}) copy-start(s32[1024]{0:T(1024)} %param.17) | copy-start | bytes 12292
  27.1 10.4 %copy-start.6 = (f32[2,128,128]{2,1,0:T(8,128)S(1)}, f32[2,128,128]{2,1,0:T(8,128)}, u32[]{:S(2)}) copy-start(f32[2,128,128]{2,1,0:T(8,128)} %stiff.3) | copy-start | bytes 393220

commit v3 on v2

v3 whole, which is shorter than its diff:
```python
import functools

import jax
import jax.numpy as jnp
from jax import lax
from jax.experimental import pallas as pl
from jax.experimental.pallas import tpu as pltpu
from jax.sharding import PartitionSpec as P

F32 = jnp.float32
BF16 = jnp.bfloat16
I32 = jnp.int32
LANES = 128
CG_STEPS = 40
CG_STOP = 1e-13
TRUE_STOP = 1e-12


def log2(value):
    assert value > 0 and value & (value - 1) == 0
    return value.bit_length() - 1


def thirds(x):
    high = x.astype(BF16).astype(F32)
    rest = x - high
    mid = rest.astype(BF16).astype(F32)
    return high, mid, rest - mid


def iota(shape, axis):
    return lax.broadcasted_iota(I32, shape, axis)


def wide(ref, first, count):
    return jnp.concatenate([ref[i : i + 1, :] for i in range(first, first + count)], axis=1)


def shifted(u):
    rows, cols = u.shape
    row, col = iota(u.shape, 0), iota(u.shape, 1)
    return (
        jnp.where(row == rows - 1, 0.0, pltpu.roll(u, rows - 1, 0)),
        jnp.where(row == 0, 0.0, pltpu.roll(u, 1, 0)),
        jnp.where(col == cols - 1, 0.0, pltpu.roll(u, cols - 1, 1)),
        jnp.where(col == 0, 0.0, pltpu.roll(u, 1, 1)),
    )


def edges(u):
    rows, cols = u.shape
    turned = u.T
    return [u[0:1, :], u[rows - 1 : rows, :], turned[0:1, :], turned[cols - 1 : cols, :]]


def pack_kernel(
    axes, disp, stiff, load, node, dest, slot, count, spin, road, active, block,
    send, trial, near, nodes, owner, slots, roads, actives, blocks,
    u, springs, loads, dests, counts, spins, sems,
):
    circs, lats = axes
    owners = send.shape[0]
    rows, cols = disp.shape[1:]
    chunks = node.shape[0]
    pairs = [
        (count, counts), (spin, spins), (node, nodes), (dest, dests), (slot, slots),
        (stiff, springs), (disp, u), (load, loads), (road, roads), (active, actives),
        (block, blocks),
    ]
    copies = [pltpu.make_async_copy(a, b, sems.at[i]) for i, (a, b) in enumerate(pairs)]
    for copy in copies:
        copy.start()
    for copy in copies[:5]:
        copy.wait()

    width = 2 * LANES if chunks % 2 == 0 else LANES
    step = width // LANES
    to, tos = [], []
    for i in range(chunks):
        live = iota((1, LANES), 1) + i * LANES < counts[0]
        target = jnp.where(live, dests[i : i + 1, :], -1)
        owner[i : i + 1, :] = target
        to.append(iota((owners, LANES), 0) == target)
        tos.append(to[i].astype(F32).astype(BF16))
    before = iota((LANES, 2 * LANES), 0) < iota((LANES, 2 * LANES), 1)
    ranks = jnp.dot(
        jnp.concatenate(tos, axis=0), before.astype(F32).astype(BF16), preferred_element_type=F32
    )
    passed = jnp.zeros((owners, LANES), F32)
    right = []
    for i in range(chunks):
        mine = ranks[i * owners : (i + 1) * owners]
        rank = jnp.sum(
            jnp.where(to[i], mine[:, :LANES] + passed, 0.0), axis=0, keepdims=True
        ).astype(I32)
        passed = passed + mine[:, LANES:]
        right.append((iota((LANES, LANES), 0) == rank).astype(F32).astype(BF16))

    for copy in copies[5:8]:
        copy.wait()
    kc = springs[0] - spins[0]
    kl = springs[1]
    diag_k = 2.0 * kc + 2.0 * kl + 0.5
    near[0] = kc
    near[1] = kl
    near[2] = diag_k
    for c in range(3):
        own = u[c]
        u_next, u_prev, u_right, u_left = shifted(own)
        force = kc * (2.0 * own - u_next - u_prev) + kl * (2.0 * own - u_right - u_left) + 0.5 * own
        trial[c] = own + (loads[c] - force) / diag_k
    table = jnp.concatenate(
        [jnp.concatenate(thirds(x), axis=1) for x in (trial[2], kc, kl)], axis=0
    ).astype(BF16)
    left = []
    for first in range(0, chunks, step):
        place = wide(nodes, first, step)
        circ = place >> log2(cols)
        lat = place & (cols - 1)
        one_lat = (iota((cols, width), 0) == lat).astype(F32).astype(BF16)
        picked = jnp.dot(
            table, jnp.concatenate([one_lat] * 3, axis=0), preferred_element_type=F32
        )
        one_circ = iota((rows, width), 0) == circ
        pieces = []
        for k in range(3):
            found = picked[k * rows : (k + 1) * rows]
            pieces += thirds(jnp.sum(jnp.where(one_circ, found, 0.0), axis=0, keepdims=True))
        where = wide(slots, first, step)
        low = where & (LANES - 1)
        pieces += [x.astype(F32) for x in (circ * cols, lat, where - low, low)]
        here = jnp.concatenate(to[first : first + step], axis=1)
        left.append(
            jnp.concatenate([jnp.where(here, x, 0.0) for x in pieces], axis=0).astype(BF16)
        )
    spread = lax.dot_general(
        jnp.concatenate(left, axis=1),
        jnp.concatenate(right, axis=1),
        (((1,), (1,)), ((), ())),
        preferred_element_type=F32,
    )
    part = [spread[i * owners : (i + 1) * owners] for i in range(13)]
    for v in range(3):
        send[:, 0, v, :] = part[3 * v] + part[3 * v + 1] + part[3 * v + 2]
    send[:, 0, 3, :] = part[9] + part[10]
    send[:, 2, 0, :] = part[11] + part[12]

    my_circ, my_lat = lax.axis_index("circ"), lax.axis_index("lat")
    me = my_circ * lats + my_lat
    after = jnp.where(my_circ == circs - 1, my_lat, me + lats)
    prior = jnp.where(my_circ == 0, (circs - 1) * lats + my_lat, me - lats)
    east = jnp.where(my_lat < lats - 1, me + 1, -1)
    west = jnp.where(my_lat > 0, me - 1, -1)
    device = iota((owners, LANES), 0)
    for c in range(3):
        layers = edges(u[c])
        lacks = jnp.zeros((owners, LANES), F32)
        for layer, reader in zip(layers, (prior, after, west, east)):
            lacks = jnp.where(device == reader, layer, lacks)
        send[:, 2, 1 + c, :] = lacks
        if c == 2:
            for t, layer in enumerate(layers):
                send[:, 1, t, :] = jnp.broadcast_to(layer, (owners, LANES))
    for copy in copies[8:]:
        copy.wait()


def column(row):
    return jnp.broadcast_to(row, (LANES, row.shape[1])).T


def patch_system(lats, got, road, active, rowed, layered):
    owners = got.shape[0]
    rows = cols = LANES
    size = 4 * LANES
    group = 16
    total = jnp.zeros((4 * group, LANES), F32)
    for first in range(0, owners, group):
        some = slice(first, first + group)
        w, kc, kl, node = [got[some, 0, v, :] for v in range(4)]
        slot = got[some, 2, 0, :].astype(I32)
        node = node.astype(I32)
        lat = node & (cols - 1)
        sender = jnp.where(kc > 0.0, iota(kc.shape, 0) + first, 0)
        pieces = thirds(w) + thirds(kc) + thirds(kl)
        pieces += tuple(x.astype(F32) for x in (node - lat, lat, sender))
        for p, piece in enumerate(pieces):
            rowed[p] = piece
        rowed[12] = (slot >> log2(LANES)).astype(F32)
        rowed[13] = (slot & (LANES - 1)).astype(F32)
        rowed[14:16] = jnp.zeros((2,) + kc.shape, F32)
        left, right = [], []
        for d in range(group):
            stack = rowed[:, d, :]
            high, low = stack[12:13, :], stack[13:14, :]
            left.append(
                jnp.concatenate(
                    [jnp.where(high == float(h), stack, 0.0) for h in range(4)], axis=0
                ).astype(BF16)
            )
            right.append(
                (iota((LANES, LANES), 0) == low.astype(I32)).astype(F32).astype(BF16)
            )
        total = total + lax.dot_general(
            jnp.concatenate(left, axis=1),
            jnp.concatenate(right, axis=1),
            (((1,), (1,)), ((), ())),
            preferred_element_type=F32,
        )
    values = []
    for at in ((0, 1, 2), (3, 4, 5), (6, 7, 8), (9, 10), (10,), (11,)):
        strips = []
        for h in range(4):
            strip = total[group * h + at[0] : group * h + at[0] + 1, :]
            for p in at[1:]:
                strip = strip + total[group * h + p : group * h + p + 1, :]
            strips.append(strip)
        values.append(jnp.concatenate(strips, axis=1))
    w, kc, kl = values[:3]
    node, lat, sender = [x.astype(I32) for x in values[3:]]
    circ = node >> log2(cols)
    after = sender + lats
    after = jnp.where(after >= owners, after - owners, after)
    before = sender - lats
    before = jnp.where(before < 0, before + owners, before)
    side = sender & (lats - 1)
    from_circ = jnp.where(
        circ == rows - 1, after, jnp.where(circ == 0, before + owners, -1)
    )
    from_lat = jnp.where(
        (lat == cols - 1) & (side < lats - 1),
        sender + 1 + 2 * owners,
        jnp.where((lat == 0) & (side > 0), sender - 1 + 3 * owners, -1),
    )
    for t in range(4):
        layered[t] = got[:, 1, t, :]
    layers = layered[...].reshape(owners * 4, LANES)
    layers = jnp.concatenate(thirds(layers), axis=1).astype(BF16)

    def pick(high, low):
        one = (iota((LANES, size), 0) == low).astype(F32).astype(BF16)
        found = jnp.dot(layers, jnp.concatenate([one] * 3, axis=0), preferred_element_type=F32)
        return jnp.sum(
            jnp.where(iota((owners * 4, size), 0) == high, found, 0.0), axis=0, keepdims=True
        )

    diag_k = 2.0 * kc + 2.0 * kl + 0.5
    w = w + (kc * pick(from_circ, lat) + kl * pick(from_lat, circ)) / diag_k
    mask = wide(active, 0, 4).astype(F32)
    return mask, mask * (w - wide(road, 0, 4)), 1.0 / diag_k


def factor_solve(block, mask, rhs, soft, work, press):
    size = rhs.shape[1]
    row = iota((size, 1), 0)
    lane = iota((1, LANES), 1)
    down = column(mask)
    for t in range(size // LANES):
        part = slice(t * LANES, (t + 1) * LANES)
        on = row == lane + t * LANES
        live = mask[:, part]
        work[:, part] = down * live * (block[:, part] + jnp.where(on, soft[:, part], 0.0)) + (
            jnp.where(on, 1.0 - live, 0.0)
        )
    work[:, size:] = column(rhs)
    place = iota((1, size), 1)

    def eliminate(j, carry):
        pivot_row = work[pl.ds(j, 1), :]
        pivot = jnp.sum(jnp.where(place == j, pivot_row[:, :size], 0.0), axis=1, keepdims=True)
        start = pl.multiple_of((j >> log2(LANES)) << log2(LANES), LANES)
        tile = work[:, pl.ds(start, LANES)]
        below = jnp.sum(jnp.where(lane == j - start, tile, 0.0), axis=1, keepdims=True)
        ratio = jnp.where(row > j, below / pivot, 0.0)
        work[...] = work[...] - ratio * pivot_row
        return carry

    lax.fori_loop(0, size, eliminate, 0)

    def substitute(step, x):
        j = size - 1 - step
        now = work[pl.ds(j, 1), :]
        upper = now[:, :size]
        pivot = jnp.sum(jnp.where(place == j, upper, 0.0), axis=1, keepdims=True)
        known = jnp.sum(upper * x, axis=1, keepdims=True)
        return jnp.where(place == j, (now[:, size : size + 1] - known) / pivot, x)

    press[...] = lax.fori_loop(0, size, substitute, jnp.zeros((1, size), F32))


def over(top, bottom):
    return jnp.where(bottom > 0.0, top / bottom, 0.0)


def dot(a, b):
    return jnp.sum(a * b, axis=1, keepdims=True)


def times(block, u, mask, soft):
    down = column(u)
    parts = [
        jnp.sum(block[:, first : first + LANES] * down, axis=0, keepdims=True)
        for first in range(0, u.shape[1], LANES)
    ]
    return mask * (jnp.concatenate(parts, axis=1) + soft * u)


def solve_kernel(
    lats, got, road, active, block, send, pressure, work, press, rowed, layered
):
    size = 4 * LANES
    mask, rhs, soft = patch_system(lats, got, road, active, rowed, layered)
    square = iota((LANES, LANES), 0) == iota((LANES, LANES), 1)
    diagonal = jnp.concatenate(
        [
            jnp.sum(
                jnp.where(square, block[i : i + LANES, i : i + LANES], 0.0), axis=0, keepdims=True
            )
            for i in range(0, size, LANES)
        ],
        axis=1,
    )
    scale = mask / (diagonal + soft)
    start = dot(rhs, scale * rhs)

    def advance(x, r, p, s, norm, alpha):
        u = scale * r
        w = times(block, u, mask, soft)
        now = dot(r, u)
        beta = over(now, norm)
        alpha = over(now, dot(w, u) - over(beta * now, alpha))
        p = u + beta * p
        s = w + beta * s
        return x + alpha * p, r - alpha * s, p, s, now, alpha

    def going(state):
        step, norm = state[0], state[5]
        return (step < CG_STEPS) & (norm[0, 0] > CG_STOP * start[0, 0])

    def body(state):
        return (state[0] + 2,) + advance(*advance(*state[1:]))

    zero = jnp.zeros((1, size), F32)
    none = jnp.zeros((1, 1), F32)
    x = lax.while_loop(going, body, (0, zero, rhs, zero, zero, start, none))[1]
    gap = rhs - times(block, x, mask, soft)
    press[...] = x

    @pl.when(jnp.logical_not(dot(gap, scale * gap)[0, 0] <= TRUE_STOP * start[0, 0]))
    def _():
        factor_solve(block, mask, rhs, soft, work, press)

    answer = press[...]
    for j in range(4):
        part = answer[:, j * LANES : (j + 1) * LANES]
        pressure[j : j + 1, :] = part
        send[:, j, :] = jnp.broadcast_to(part, (send.shape[0], LANES))


def finish_kernel(axes, trial, near, node, owner, slot, got, back, out):
    circs, lats = axes
    owners = got.shape[0]
    rows, cols = trial.shape[1:]
    chunks = node.shape[0]
    my_circ, my_lat = lax.axis_index("circ"), lax.axis_index("lat")
    me = my_circ * lats + my_lat
    after = jnp.where(my_circ == circs - 1, my_lat, me + lats)
    before = jnp.where(my_circ == 0, (circs - 1) * lats + my_lat, me - lats)
    right_dev = jnp.minimum(me + 1, owners - 1)
    left_dev = jnp.maximum(me - 1, 0)
    kc, kl, diag_k = near[0], near[1], near[2]
    row, col = iota((rows, cols), 0), iota((rows, cols), 1)
    for c in range(3):
        down, up = got[after, 2, 1 + c : 2 + c, :], got[before, 2, 1 + c : 2 + c, :]
        east, west = got[right_dev, 2, 1 + c : 2 + c, :], got[left_dev, 2, 1 + c : 2 + c, :]
        east = jnp.where(my_lat < lats - 1, east, 0.0)
        west = jnp.where(my_lat > 0, west, 0.0)
        circ_in = jnp.where(row == rows - 1, down, jnp.where(row == 0, up, 0.0))
        lat_in = jnp.where(
            col == cols - 1, column(east), jnp.where(col == 0, column(west), 0.0)
        )
        out[c] = trial[c] + (kc * circ_in + kl * lat_in) / diag_k

    answers = jnp.concatenate([back[:, j, :] for j in range(4)], axis=0)
    answers = jnp.concatenate(thirds(answers), axis=1).astype(BF16)
    step = 2 if chunks % 2 == 0 else 1
    span = step * LANES
    left, right = [], []
    for first in range(0, chunks, step):
        nodes = wide(node, first, step)
        where = wide(slot, first, step)
        device = wide(owner, first, step)
        low = where & (LANES - 1)
        source = jnp.where(device < 0, -1, (where >> log2(LANES)) * owners + device)
        one_low = (iota((LANES, span), 0) == low).astype(F32).astype(BF16)
        found = jnp.dot(
            answers, jnp.concatenate([one_low] * 3, axis=0), preferred_element_type=F32
        )
        push = jnp.sum(
            jnp.where(iota((4 * owners, span), 0) == source, found, 0.0), axis=0, keepdims=True
        )
        one_circ = iota((rows, span), 0) == nodes >> log2(cols)
        left.append(
            jnp.concatenate(
                [jnp.where(one_circ, x, 0.0) for x in thirds(push)], axis=0
            ).astype(BF16)
        )
        right.append((iota((cols, span), 0) == (nodes & (cols - 1))).astype(F32).astype(BF16))
    force = lax.dot_general(
        jnp.concatenate(left, axis=1),
        jnp.concatenate(right, axis=1),
        (((1,), (1,)), ((), ())),
        preferred_element_type=F32,
    )
    force = force[:rows] + force[rows : 2 * rows] + force[2 * rows :]
    out[2] = out[2] - force / diag_k


def shards(
    disp, stiff, spin, load, foot_node, foot_dest, foot_slot, foot_count, road, active, influence
):
    circs, lats = lax.axis_size("circ"), lax.axis_size("lat")
    owners = circs * lats
    size = road.shape[0]
    rows, cols = disp.shape[1:]
    assert rows == cols == LANES and size == 4 * LANES and circs > 2 and owners % 16 == 0
    anywhere = pl.BlockSpec(memory_space=pl.ANY)
    block = pl.BlockSpec(memory_space=pltpu.VMEM)
    params = pltpu.CompilerParams(vmem_limit_bytes=32 * 1024 * 1024)
    lists = [x.reshape(-1, LANES) for x in (foot_node, foot_dest, foot_slot)]
    listed = jax.ShapeDtypeStruct(lists[0].shape, I32)
    strip = (4, LANES)
    send, trial, near, nodes, owner, slots, roads, actives, blocks = pl.pallas_call(
        functools.partial(pack_kernel, (circs, lats)),
        in_specs=[anywhere] * 11,
        out_specs=[block] * 9,
        out_shape=[
            jax.ShapeDtypeStruct((owners, 3, 4, LANES), F32),
            jax.ShapeDtypeStruct((3, rows, cols), F32),
            jax.ShapeDtypeStruct((3, rows, cols), F32),
            listed,
            listed,
            listed,
            jax.ShapeDtypeStruct(strip, F32),
            jax.ShapeDtypeStruct(strip, I32),
            jax.ShapeDtypeStruct((size, size), F32),
        ],
        scratch_shapes=[
            pltpu.VMEM((3, rows, cols), F32),
            pltpu.VMEM((2, rows, cols), F32),
            pltpu.VMEM((3, rows, cols), F32),
            pltpu.VMEM(lists[0].shape, I32),
            pltpu.SMEM((1,), I32),
            pltpu.SMEM((1,), F32),
            pltpu.SemaphoreType.DMA((11,)),
        ],
        compiler_params=params,
        name="pack_rows",
    )(
        disp, stiff, load, *lists, foot_count, spin,
        road.reshape(strip), active.reshape(strip), influence[0],
    )
    got = lax.all_to_all(send, ("circ", "lat"), split_axis=0, concat_axis=0, tiled=True)
    reply, pressure = pl.pallas_call(
        functools.partial(solve_kernel, lats),
        in_specs=[block] * 4,
        out_specs=[block, block],
        out_shape=[
            jax.ShapeDtypeStruct((owners,) + strip, F32),
            jax.ShapeDtypeStruct(strip, F32),
        ],
        scratch_shapes=[
            pltpu.VMEM((size, size + LANES), F32),
            pltpu.VMEM((1, size), F32),
            pltpu.VMEM((16, 16, LANES), F32),
            pltpu.VMEM((4, owners, LANES), F32),
        ],
        compiler_params=params,
        name="solve_patch",
    )(got, roads, actives, blocks)
    back = lax.all_to_all(reply, ("circ", "lat"), split_axis=0, concat_axis=0, tiled=True)
    new_disp = pl.pallas_call(
        functools.partial(finish_kernel, (circs, lats)),
        in_specs=[block] * 7,
        out_specs=block,
        out_shape=jax.ShapeDtypeStruct(disp.shape, F32),
        compiler_params=params,
        name="finish_nodes",
    )(trial, near, nodes, owner, slots, got, back)
    return (new_disp, pressure.reshape(size))


def solution(mesh):
    return jax.shard_map(
        shards,
        mesh=mesh,
        in_specs=(
            P(None, ("cases", "circ"), "lat"),
            P(None, ("cases", "circ"), "lat"),
            P("cases"),
            P(None, ("cases", "circ"), "lat"),
            P(("cases", "circ", "lat")),
            P(("cases", "circ", "lat")),
            P(("cases", "circ", "lat")),
            P(("cases", "circ", "lat")),
            P(("cases", "circ", "lat")),
            P(("cases", "circ", "lat")),
            P(("cases", "circ", "lat"), None, None),
        ),
        out_specs=(P(None, ("cases", "circ"), "lat"), P(("cases", "circ", "lat"))),
        check_vma=False,
    )
```

time: 39.3 us -> 38.4 us (0.977)
  blocking collectives: 25.7 us -> 23.3 us
  Pallas kernels: 5.78 us -> 7.3 us
    all_to_all x1, blocking collectives: 10.4 us -> 9.15 us  [shards(): lax.all_to_all(reply, ('circ', 'lat'), split_axis=0, concat_axis=0, tiled...]
    pallas_call x1, Pallas kernels: 1.05 us -> 2.18 us  [shards(): pl.pallas_call(functools.partial(pack_kernel, (circs, lats)), in_specs=[a...]
    all_to_all x1, blocking collectives: 15.3 us -> 14.2 us  [shards(): lax.all_to_all(send, ('circ', 'lat'), split_axis=0, concat_axis=0, tiled=...]
    pallas_call x1, Pallas kernels: 3.38 us -> 3.87 us  [shards(): pl.pallas_call(functools.partial(solve_kernel, lats), in_specs=[block] *...]
    unnamed x26 -> x18, local copies, waits for them, and re-layouts: 5.39 us -> 5.34 us
where the time goes in v3:
time: 38.4 us; the launch traced here: 38 us
  blocking collectives  23.3 us (61%)
  Pallas kernels  7.3 us (19%)
  local copies, waits for them, and re-layouts  5.34 us (14%)
  between operations  2.01 us (5%)
    all_to_all x1, blocking collectives, shards(): lax.all_to_all(send, ('circ', 'lat'), split_axis=0, concat_axis=0, tiled=...  14.2 us
    all_to_all x1, blocking collectives, shards(): lax.all_to_all(reply, ('circ', 'lat'), split_axis=0, concat_axis=0, tiled...  9.15 us
    unnamed x18, local copies, waits for them, and re-layouts  5.34 us
    pallas_call x1, Pallas kernels, shards(): pl.pallas_call(functools.partial(solve_kernel, lats), in_specs=[block] *...  3.87 us
    pallas_call x1, Pallas kernels, shards(): pl.pallas_call(functools.partial(pack_kernel, (circs, lats)), in_specs=[a...  2.18 us
    pallas_call x1, Pallas kernels, shards(): pl.pallas_call(functools.partial(finish_kernel, (circs, lats)), in_specs=...  1.25 us

profile of v3, /device:TPU:0, one launch (start us, length us, event | category | flops | bytes accessed | tf_op | source)
XLA Modules:
  0.0 38.0 jit_solution(3556191325796594399)
XLA Ops:
  0.6 0.0 copy-start.7
  1.3 0.0 copy-start.6
  2.0 0.0 copy-start.5
  2.0 0.0 copy-start.4
  2.0 0.0 copy-done.7
  2.0 0.0 copy-done.6
  2.0 0.6 %copy-done.5 = s32[1024]{0:T(1024)S(1)} copy-done((s32[1024]{0:T(1024)S(1)}, s32[1024]{0:T(1024)}, u32[]{:S(2)}) %copy-start.5) | copy-done | bytes 4120
  2.7 0.0 copy-done.4
  2.7 0.0 copy-start
  2.7 1.2 %copy-done = f32[1,512,512]{2,1,0:T(8,128)S(1)} copy-done((f32[1,512,512]{2,1,0:T(8,128)S(1)}, f32[1,512,512]{2,1,0:T(8,128)}, u32[]{:S(2)}) %copy-start) | copy-done | bytes 1048600
  3.9 0.0 copy-start.1
  3.9 0.9 %copy-done.1 = f32[3,128,128]{2,1,0:T(8,128)S(1)} copy-done((f32[3,128,128]{2,1,0:T(8,128)S(1)}, f32[3,128,128]{2,1,0:T(8,128)}, u32[]{:S(2)}) %copy-start.1) | copy-done | bytes 196632
  4.8 0.0 copy-start.2
  4.8 0.9 %copy-done.2 = f32[3,128,128]{2,1,0:T(8,128)S(1)} copy-done((f32[3,128,128]{2,1,0:T(8,128)S(1)}, f32[3,128,128]{2,1,0:T(8,128)}, u32[]{:S(2)}) %copy-start.2) | copy-done | bytes 196632
  5.8 0.0 copy-start.3
  5.8 0.9 %copy-done.3 = f32[2,128,128]{2,1,0:T(8,128)S(1)} copy-done((f32[2,128,128]{2,1,0:T(8,128)S(1)}, f32[2,128,128]{2,1,0:T(8,128)}, u32[]{:S(2)}) %copy-start.3) | copy-done | bytes 131096
  6.7 0.0 copy-start.8
  6.7 0.7 %copy-done.8 = s32[512]{0:T(512)S(1)} copy-done((s32[512]{0:T(512)S(1)}, s32[512]{0:T(512)}, u32[]{:S(2)}) %copy-start.8) | copy-done | bytes 2072
  7.3 2.2 %pack_rows.1 = (f32[16,3,4,128]{3,2,1,0:T(4,128)S(1)}, f32[3,128,128]{2,1,0:T(8,128)S(1)}, f32[3,128,128]{2,1,0:T(8,128)S(1)}, s32[8,128]{1,0:T(8,128)S(1)}, s32...) custom-call(f32[3,128,128]{2,1,0:T(8,128)S(1)} %copy-done.1, ...), custom_call_target="tpu_custom_call" | custom-call | tf_op jit(solution)/shard_map/pack_rows/pallas_call | solution.py:433
  9.5 14.2 %all_to_all.10.got = f32[16,3,4,128]{3,2,1,0:T(4,128)S(1)} all-to-all(f32[16,3,4,128]{3,2,1,0:T(4,128)S(1)} %get-tuple-element.18), channel_id=1, replica_groups=mesh['cases'=2,'circ'=4,'lat'=4] {'circ','lat'}, dimensions={0} | all-to-all | bytes 196608 | tf_op jit(solution)/shard_map/all_to_all | solution.py:463
  23.7 3.9 %solve_patch.1 = (f32[16,4,128]{2,1,0:T(4,128)S(1)}, f32[4,128]{1,0:T(4,128)}) custom-call(f32[16,3,4,128]{3,2,1,0:T(4,128)S(1)} %all_to_all.10.got, f32[4,128]{1,0:T(4,128)S(1)} %get-tuple-element.19.road, s32[4,128]{1,0:T(4,128)S(1)} %get-tuple-element.20.active, f32[512,512]{1,0:T(8,128)S(1)} %get-tuple-element.21.block), custom_call_target="tpu_custom_call" | custom-call | tf_op jit(solution)/shard_map/solve_patch/pallas_call | solution.py:464
  27.6 9.2 %all_to_all.11.back = f32[16,4,128]{2,1,0:T(4,128)S(1)} all-to-all(f32[16,4,128]{2,1,0:T(4,128)S(1)} %get-tuple-element.22), channel_id=1, replica_groups=mesh['cases'=2,'circ'=4,'lat'=4] {'circ','lat'}, dimensions={0} | all-to-all | bytes 65536 | tf_op jit(solution)/shard_map/all_to_all | solution.py:481
  36.7 1.2 %finish_nodes.1 = f32[3,128,128]{2,1,0:T(8,128)} custom-call(f32[3,128,128]{2,1,0:T(8,128)S(1)} %get-tuple-element.13.trial, f32[3,128,128]{2,1,0:T(8,128)S(1)} %get-tuple-element.14.near, s32[8,128]{1,0:T(8,128)S(1)} %get-tuple-element.15.node, s32[8,128]{1,0:T(8,128)S(1)} %get-tuple-element.16.owner, s32[8,128]{1,0:T(8,128)S(1)} %get-tuple-element.17.slot, ...), custom_call_target="tpu_custom_call" | custom-call | tf_op jit(solution)/shard_map/finish_nodes/pallas_call | solution.py:482
Async XLA Ops:
  0.6 1.4 %copy-start.7 = (f32[512]{0:T(512)S(1)}, f32[512]{0:T(512)}, u32[]{:S(2)}) copy-start(f32[512]{0:T(512)} %param.19) | copy-start | bytes 6148
  1.3 0.7 %copy-start.6 = (s32[1024]{0:T(1024)S(1)}, s32[1024]{0:T(1024)}, u32[]{:S(2)}) copy-start(s32[1024]{0:T(1024)} %param.17) | copy-start | bytes 12292
  2.0 0.7 %copy-start.5 = (s32[1024]{0:T(1024)S(1)}, s32[1024]{0:T(1024)}, u32[]{:S(2)}) copy-start(s32[1024]{0:T(1024)} %param.16) | copy-start | bytes 12292
  2.0 0.7 %copy-start.4 = (s32[1024]{0:T(1024)S(1)}, s32[1024]{0:T(1024)}, u32[]{:S(2)}) copy-start(s32[1024]{0:T(1024)} %param.15) | copy-start | bytes 12292
  2.7 1.2 %copy-start = (f32[1,512,512]{2,1,0:T(8,128)S(1)}, f32[1,512,512]{2,1,0:T(8,128)}, u32[]{:S(2)}) copy-start(f32[1,512,512]{2,1,0:T(8,128)} %param.21) | copy-start | bytes 3145732
  3.9 0.9 %copy-start.1 = (f32[3,128,128]{2,1,0:T(8,128)S(1)}, f32[3,128,128]{2,1,0:T(8,128)}, u32[]{:S(2)}) copy-start(f32[3,128,128]{2,1,0:T(8,128)} %disp.1) | copy-start | bytes 589828
  4.8 0.9 %copy-start.2 = (f32[3,128,128]{2,1,0:T(8,128)S(1)}, f32[3,128,128]{2,1,0:T(8,128)}, u32[]{:S(2)}) copy-start(f32[3,128,128]{2,1,0:T(8,128)} %load.1) | copy-start | bytes 589828
  5.8 0.9 %copy-start.3 = (f32[2,128,128]{2,1,0:T(8,128)S(1)}, f32[2,128,128]{2,1,0:T(8,128)}, u32[]{:S(2)}) copy-start(f32[2,128,128]{2,1,0:T(8,128)} %stiff.1) | copy-start | bytes 393220
  6.7 0.7 %copy-start.8 = (s32[512]{0:T(512)S(1)}, s32[512]{0:T(512)}, u32[]{:S(2)}) copy-start(s32[512]{0:T(512)} %param.20) | copy-start | bytes 6148

commit v4 on v3

--- a/solution.py
+++ b/solution.py
@@ -54,30 +54,29 @@
 
 
 def pack_kernel(
-    axes, disp, stiff, load, node, dest, slot, count, spin, road, active, block,
+    axes, count, spin, node, dest, slot, stiff, disp, load, road, active, block,
     send, trial, near, nodes, owner, slots, roads, actives, blocks,
-    u, springs, loads, dests, counts, spins, sems,
+    u, springs, loads, dests, sems,
 ):
     circs, lats = axes
     owners = send.shape[0]
     rows, cols = disp.shape[1:]
     chunks = node.shape[0]
     pairs = [
-        (count, counts), (spin, spins), (node, nodes), (dest, dests), (slot, slots),
-        (stiff, springs), (disp, u), (load, loads), (road, roads), (active, actives),
+        (node, nodes), (dest, dests), (slot, slots), (stiff, springs), (disp, u), (load, loads), (road, roads), (active, actives),
         (block, blocks),
     ]
     copies = [pltpu.make_async_copy(a, b, sems.at[i]) for i, (a, b) in enumerate(pairs)]
     for copy in copies:
         copy.start()
-    for copy in copies[:5]:
+    for copy in copies[:3]:
         copy.wait()
 
     width = 2 * LANES if chunks % 2 == 0 else LANES
     step = width // LANES
     to, tos = [], []
     for i in range(chunks):
-        live = iota((1, LANES), 1) + i * LANES < counts[0]
+        live = iota((1, LANES), 1) + i * LANES < count[0]
         target = jnp.where(live, dests[i : i + 1, :], -1)
         owner[i : i + 1, :] = target
         to.append(iota((owners, LANES), 0) == target)
@@ -96,9 +95,9 @@
         passed = passed + mine[:, LANES:]
         right.append((iota((LANES, LANES), 0) == rank).astype(F32).astype(BF16))
 
-    for copy in copies[5:8]:
+    for copy in copies[3:6]:
         copy.wait()
-    kc = springs[0] - spins[0]
+    kc = springs[0] - spin[0]
     kl = springs[1]
     diag_k = 2.0 * kc + 2.0 * kl + 0.5
     near[0] = kc
@@ -161,7 +160,7 @@
         if c == 2:
             for t, layer in enumerate(layers):
                 send[:, 1, t, :] = jnp.broadcast_to(layer, (owners, LANES))
-    for copy in copies[8:]:
+    for copy in copies[6:]:
         copy.wait()
 
 
@@ -424,7 +423,7 @@
     size = road.shape[0]
     rows, cols = disp.shape[1:]
     assert rows == cols == LANES and size == 4 * LANES and circs > 2 and owners % 16 == 0
-    anywhere = pl.BlockSpec(memory_space=pl.ANY)
+    anywhere = pl.BlockSpec(memory_space=pltpu.HBM)
     block = pl.BlockSpec(memory_space=pltpu.VMEM)
     params = pltpu.CompilerParams(vmem_limit_bytes=32 * 1024 * 1024)
     lists = [x.reshape(-1, LANES) for x in (foot_node, foot_dest, foot_slot)]
@@ -432,7 +431,7 @@
     strip = (4, LANES)
     send, trial, near, nodes, owner, slots, roads, actives, blocks = pl.pallas_call(
         functools.partial(pack_kernel, (circs, lats)),
-        in_specs=[anywhere] * 11,
+        in_specs=[pl.BlockSpec(memory_space=pltpu.SMEM)] * 2 + [anywhere] * 9,
         out_specs=[block] * 9,
         out_shape=[
             jax.ShapeDtypeStruct((owners, 3, 4, LANES), F32),
@@ -450,15 +449,18 @@
             pltpu.VMEM((2, rows, cols), F32),
             pltpu.VMEM((3, rows, cols), F32),
             pltpu.VMEM(lists[0].shape, I32),
-            pltpu.SMEM((1,), I32),
-            pltpu.SMEM((1,), F32),
-            pltpu.SemaphoreType.DMA((11,)),
+            pltpu.SemaphoreType.DMA((9,)),
         ],
         compiler_params=params,
         name="pack_rows",
     )(
-        disp, stiff, load, *lists, foot_count, spin,
-        road.reshape(strip), active.reshape(strip), influence[0],
+        foot_count, spin,
+        *[
+            pltpu.with_memory_space_constraint(x, pltpu.HBM)
+            for x in (
+                *lists, stiff, disp, load, road.reshape(strip), active.reshape(strip), influence[0]
+            )
+        ]
     )
     got = lax.all_to_all(send, ("circ", "lat"), split_axis=0, concat_axis=0, tiled=True)
     reply, pressure = pl.pallas_call(

time: 38.4 us -> 32.8 us (0.85)
  local copies, waits for them, and re-layouts: 5.34 us -> 0 us
    unnamed x18 -> x0, local copies, waits for them, and re-layouts: 5.34 us -> none
where the time goes in v4:
time: 32.8 us; the launch traced here: 32.5 us
  blocking collectives  23.3 us (71%)
  Pallas kernels  7.29 us (22%)
  between operations  1.93 us (6%)
    all_to_all x1, blocking collectives, shards(): lax.all_to_all(send, ('circ', 'lat'), split_axis=0, concat_axis=0, tiled=...  14.2 us
    all_to_all x1, blocking collectives, shards(): lax.all_to_all(reply, ('circ', 'lat'), split_axis=0, concat_axis=0, tiled...  9.15 us
    pallas_call x1, Pallas kernels, shards(): pl.pallas_call(functools.partial(solve_kernel, lats), in_specs=[block] *...  3.87 us
    pallas_call x1, Pallas kernels, shards(): pl.pallas_call(functools.partial(pack_kernel, (circs, lats)), in_specs=[p...  2.17 us
    pallas_call x1, Pallas kernels, shards(): pl.pallas_call(functools.partial(finish_kernel, (circs, lats)), in_specs=...  1.25 us

profile of v4, /device:TPU:0, one launch (start us, length us, event | category | flops | bytes accessed | tf_op | source)
XLA Modules:
  0.0 32.5 jit_solution(8707429392530675858)
XLA Ops:
  1.9 2.2 %pack_rows.1 = (f32[16,3,4,128]{3,2,1,0:T(4,128)S(1)}, f32[3,128,128]{2,1,0:T(8,128)S(1)}, f32[3,128,128]{2,1,0:T(8,128)S(1)}, s32[8,128]{1,0:T(8,128)S(1)}, s32...) custom-call(s32[1]{0:T(128)S(6)} %copy.14.count, ...), custom_call_target="tpu_custom_call" | custom-call | tf_op jit(solution)/shard_map/pack_rows/pallas_call | solution.py:432
  4.1 14.2 %all_to_all.10.got = f32[16,3,4,128]{3,2,1,0:T(4,128)S(1)} all-to-all(f32[16,3,4,128]{3,2,1,0:T(4,128)S(1)} %get-tuple-element.18), channel_id=1, replica_groups=mesh['cases'=2,'circ'=4,'lat'=4] {'circ','lat'}, dimensions={0} | all-to-all | bytes 196608 | tf_op jit(solution)/shard_map/all_to_all | solution.py:465
  18.3 3.9 %solve_patch.1 = (f32[16,4,128]{2,1,0:T(4,128)S(1)}, f32[4,128]{1,0:T(4,128)}) custom-call(f32[16,3,4,128]{3,2,1,0:T(4,128)S(1)} %all_to_all.10.got, f32[4,128]{1,0:T(4,128)S(1)} %get-tuple-element.19.road, s32[4,128]{1,0:T(4,128)S(1)} %get-tuple-element.20.active, f32[512,512]{1,0:T(8,128)S(1)} %get-tuple-element.21.block), custom_call_target="tpu_custom_call" | custom-call | tf_op jit(solution)/shard_map/solve_patch/pallas_call | solution.py:466
  22.1 9.2 %all_to_all.11.back = f32[16,4,128]{2,1,0:T(4,128)S(1)} all-to-all(f32[16,4,128]{2,1,0:T(4,128)S(1)} %get-tuple-element.22), channel_id=1, replica_groups=mesh['cases'=2,'circ'=4,'lat'=4] {'circ','lat'}, dimensions={0} | all-to-all | bytes 65536 | tf_op jit(solution)/shard_map/all_to_all | solution.py:483
  31.3 1.2 %finish_nodes.1 = f32[3,128,128]{2,1,0:T(8,128)} custom-call(f32[3,128,128]{2,1,0:T(8,128)S(1)} %get-tuple-element.13.trial, f32[3,128,128]{2,1,0:T(8,128)S(1)} %get-tuple-element.14.near, s32[8,128]{1,0:T(8,128)S(1)} %get-tuple-element.15.node, s32[8,128]{1,0:T(8,128)S(1)} %get-tuple-element.16.owner, s32[8,128]{1,0:T(8,128)S(1)} %get-tuple-element.17.slot, ...), custom_call_target="tpu_custom_call" | custom-call | tf_op jit(solution)/shard_map/finish_nodes/pallas_call | solution.py:484

commit v5 on v4

--- a/solution.py
+++ b/solution.py
@@ -11,6 +11,8 @@
 BF16 = jnp.bfloat16
 I32 = jnp.int32
 LANES = 128
+CG_FIRST = 3
+CG_AGAIN = 4
 CG_STEPS = 40
 CG_STOP = 1e-13
 TRUE_STOP = 1e-12
@@ -296,11 +298,14 @@
 
 
 def times(block, u, mask, soft):
-    down = column(u)
-    parts = [
-        jnp.sum(block[:, first : first + LANES] * down, axis=0, keepdims=True)
-        for first in range(0, u.shape[1], LANES)
-    ]
+    size = u.shape[1]
+    parts = [jnp.zeros((8, LANES), F32)] * (size // LANES)
+    for i in range(0, size, LANES):
+        down = column(u[:, i : i + LANES])
+        for k in range(size // LANES):
+            tile = block[i : i + LANES, k * LANES : (k + 1) * LANES] * down
+            parts[k] = parts[k] + jnp.sum(tile.reshape(LANES // 8, 8, LANES), axis=0)
+    parts = [jnp.sum(part, axis=0, keepdims=True) for part in parts]
     return mask * (jnp.concatenate(parts, axis=1) + soft * u)
 
 
@@ -321,39 +326,64 @@
     )
     scale = mask / (diagonal + soft)
     start = dot(rhs, scale * rhs)
-
-    def advance(x, r, p, s, norm, alpha):
+    zero = jnp.zeros((1, size), F32)
+    none = jnp.zeros((1, 1), F32)
+
+    def begin(x, r):
         u = scale * r
-        w = times(block, u, mask, soft)
+        return x, r, u, times(block, u, mask, soft), zero, zero, zero, zero, none, none
+
+    def advance(x, r, u, w, z, q, s, p, norm, alpha):
+        m = scale * w
+        n = times(block, m, mask, soft)
         now = dot(r, u)
         beta = over(now, norm)
         alpha = over(now, dot(w, u) - over(beta * now, alpha))
+        z = n + beta * z
+        q = m + beta * q
+        s = w + beta * s
         p = u + beta * p
-        s = w + beta * s
-        return x + alpha * p, r - alpha * s, p, s, now, alpha
-
-    def going(state):
-        step, norm = state[0], state[5]
-        return (step < CG_STEPS) & (norm[0, 0] > CG_STOP * start[0, 0])
-
-    def body(state):
-        return (state[0] + 2,) + advance(*advance(*state[1:]))
-
-    zero = jnp.zeros((1, size), F32)
-    none = jnp.zeros((1, 1), F32)
-    x = lax.while_loop(going, body, (0, zero, rhs, zero, zero, start, none))[1]
-    gap = rhs - times(block, x, mask, soft)
-    press[...] = x
-
-    @pl.when(jnp.logical_not(dot(gap, scale * gap)[0, 0] <= TRUE_STOP * start[0, 0]))
+        x, r, u, w = x + alpha * p, r - alpha * s, u - alpha * q, w - alpha * z
+        return x, r, u, w, z, q, s, p, now, alpha
+
+    def finish(x):
+        press[...] = x
+        for j in range(4):
+            part = x[:, j * LANES : (j + 1) * LANES]
+            pressure[j : j + 1, :] = part
+            send[:, j, :] = jnp.broadcast_to(part, (send.shape[0], LANES))
+
+    def gap(x):
+        return rhs - times(block, x, mask, soft)
+
+    def small(r):
+        return dot(r, scale * r)[0, 0] <= TRUE_STOP * start[0, 0]
+
+    state = begin(zero, rhs)
+    for _ in range(CG_FIRST):
+        state = advance(*state)
+    state = begin(state[0], gap(state[0]))
+    for _ in range(CG_AGAIN):
+        state = advance(*state)
+    first, rest = state[:2]
+    finish(first)
+
+    @pl.when(jnp.logical_not(small(rest)))
     def _():
-        factor_solve(block, mask, rhs, soft, work, press)
-
-    answer = press[...]
-    for j in range(4):
-        part = answer[:, j * LANES : (j + 1) * LANES]
-        pressure[j : j + 1, :] = part
-        send[:, j, :] = jnp.broadcast_to(part, (send.shape[0], LANES))
+        def going(state):
+            step, norm = state[0], state[9]
+            return (step < CG_STEPS) & ((step == 0) | (norm[0, 0] > CG_STOP * start[0, 0]))
+
+        def body(state):
+            return (state[0] + 1,) + advance(*state[1:])
+
+        x = lax.while_loop(going, body, (0,) + begin(first, gap(first)))[1]
+        finish(x)
+
+        @pl.when(jnp.logical_not(small(gap(x))))
+        def _():
+            factor_solve(block, mask, rhs, soft, work, press)
+            finish(press[...])
 
 
 def finish_kernel(axes, trial, near, node, owner, slot, got, back, out):

time: 32.8 us -> 32 us (0.976)
  Pallas kernels: 7.29 us -> 6.53 us
    pallas_call x1, Pallas kernels: 3.87 us -> 3.12 us  [shards(): pl.pallas_call(functools.partial(solve_kernel, lats), in_specs=[block] *...]
where the time goes in v5:
time: 32 us; the launch traced here: 31.8 us
  blocking collectives  23.3 us (73%)
  Pallas kernels  6.53 us (20%)
  between operations  1.93 us (6%)
    all_to_all x1, blocking collectives, shards(): lax.all_to_all(send, ('circ', 'lat'), split_axis=0, concat_axis=0, tiled=...  14.2 us
    all_to_all x1, blocking collectives, shards(): lax.all_to_all(reply, ('circ', 'lat'), split_axis=0, concat_axis=0, tiled...  9.15 us
    pallas_call x1, Pallas kernels, shards(): pl.pallas_call(functools.partial(solve_kernel, lats), in_specs=[block] *...  3.12 us
    pallas_call x1, Pallas kernels, shards(): pl.pallas_call(functools.partial(pack_kernel, (circs, lats)), in_specs=[p...  2.17 us
    pallas_call x1, Pallas kernels, shards(): pl.pallas_call(functools.partial(finish_kernel, (circs, lats)), in_specs=...  1.25 us

profile of v5, /device:TPU:0, one launch (start us, length us, event | category | flops | bytes accessed | tf_op | source)
XLA Modules:
  0.0 31.8 jit_solution(16322936346287585554)
XLA Ops:
  1.9 2.2 %pack_rows.1 = (f32[16,3,4,128]{3,2,1,0:T(4,128)S(1)}, f32[3,128,128]{2,1,0:T(8,128)S(1)}, f32[3,128,128]{2,1,0:T(8,128)S(1)}, s32[8,128]{1,0:T(8,128)S(1)}, s32...) custom-call(s32[1]{0:T(128)S(6)} %copy.14.count, ...), custom_call_target="tpu_custom_call" | custom-call | tf_op jit(solution)/shard_map/pack_rows/pallas_call | solution.py:462
  4.1 14.2 %all_to_all.10.got = f32[16,3,4,128]{3,2,1,0:T(4,128)S(1)} all-to-all(f32[16,3,4,128]{3,2,1,0:T(4,128)S(1)} %get-tuple-element.18), channel_id=1, replica_groups=mesh['cases'=2,'circ'=4,'lat'=4] {'circ','lat'}, dimensions={0} | all-to-all | bytes 196608 | tf_op jit(solution)/shard_map/all_to_all | solution.py:495
  18.3 3.1 %solve_patch.1 = (f32[16,4,128]{2,1,0:T(4,128)S(1)}, f32[4,128]{1,0:T(4,128)}) custom-call(f32[16,3,4,128]{3,2,1,0:T(4,128)S(1)} %all_to_all.10.got, f32[4,128]{1,0:T(4,128)S(1)} %get-tuple-element.19.road, s32[4,128]{1,0:T(4,128)S(1)} %get-tuple-element.20.active, f32[512,512]{1,0:T(8,128)S(1)} %get-tuple-element.21.block), custom_call_target="tpu_custom_call" | custom-call | tf_op jit(solution)/shard_map/solve_patch/pallas_call | solution.py:496
  21.4 9.2 %all_to_all.11.back = f32[16,4,128]{2,1,0:T(4,128)S(1)} all-to-all(f32[16,4,128]{2,1,0:T(4,128)S(1)} %get-tuple-element.22), channel_id=1, replica_groups=mesh['cases'=2,'circ'=4,'lat'=4] {'circ','lat'}, dimensions={0} | all-to-all | bytes 65536 | tf_op jit(solution)/shard_map/all_to_all | solution.py:513
  30.5 1.2 %finish_nodes.1 = f32[3,128,128]{2,1,0:T(8,128)} custom-call(f32[3,128,128]{2,1,0:T(8,128)S(1)} %get-tuple-element.13.trial, f32[3,128,128]{2,1,0:T(8,128)S(1)} %get-tuple-element.14.near, s32[8,128]{1,0:T(8,128)S(1)} %get-tuple-element.15.node, s32[8,128]{1,0:T(8,128)S(1)} %get-tuple-element.16.owner, s32[8,128]{1,0:T(8,128)S(1)} %get-tuple-element.17.slot, ...), custom_call_target="tpu_custom_call" | custom-call | tf_op jit(solution)/shard_map/finish_nodes/pallas_call | solution.py:514

commit v6 on v5

--- a/solution.py
+++ b/solution.py
@@ -14,8 +14,8 @@
 CG_FIRST = 3
 CG_AGAIN = 4
 CG_STEPS = 40
-CG_STOP = 1e-13
-TRUE_STOP = 1e-12
+CG_STOP = 2e-14
+TRUE_STOP = 4e-13
 
 
 def log2(value):
@@ -382,8 +382,11 @@
 
         @pl.when(jnp.logical_not(small(gap(x))))
         def _():
-            factor_solve(block, mask, rhs, soft, work, press)
-            finish(press[...])
+            def refine(step, x):
+                factor_solve(block, mask, gap(x), soft, work, press)
+                return x + press[...]
+
+            finish(lax.fori_loop(0, 2, refine, zero))
 
 
 def finish_kernel(axes, trial, near, node, owner, slot, got, back, out):

time: 32 us -> 32 us (level)
  no operation moved by 1% of the time
where the time goes in v6:
time: 32 us; the launch traced here: 31.8 us
  blocking collectives  23.3 us (73%)
  Pallas kernels  6.53 us (20%)
  between operations  1.93 us (6%)
    all_to_all x1, blocking collectives, shards(): lax.all_to_all(send, ('circ', 'lat'), split_axis=0, concat_axis=0, tiled=...  14.2 us
    all_to_all x1, blocking collectives, shards(): lax.all_to_all(reply, ('circ', 'lat'), split_axis=0, concat_axis=0, tiled...  9.15 us
    pallas_call x1, Pallas kernels, shards(): pl.pallas_call(functools.partial(solve_kernel, lats), in_specs=[block] *...  3.12 us
    pallas_call x1, Pallas kernels, shards(): pl.pallas_call(functools.partial(pack_kernel, (circs, lats)), in_specs=[p...  2.17 us
    pallas_call x1, Pallas kernels, shards(): pl.pallas_call(functools.partial(finish_kernel, (circs, lats)), in_specs=...  1.25 us

profile of v6, /device:TPU:0, one launch (start us, length us, event | category | flops | bytes accessed | tf_op | source)
XLA Modules:
  0.0 31.8 jit_solution(3451071398096370320)
XLA Ops:
  1.9 2.2 %pack_rows.1 = (f32[16,3,4,128]{3,2,1,0:T(4,128)S(1)}, f32[3,128,128]{2,1,0:T(8,128)S(1)}, f32[3,128,128]{2,1,0:T(8,128)S(1)}, s32[8,128]{1,0:T(8,128)S(1)}, s32...) custom-call(s32[1]{0:T(128)S(6)} %copy.14.count, ...), custom_call_target="tpu_custom_call" | custom-call | tf_op jit(solution)/shard_map/pack_rows/pallas_call | solution.py:465
  4.1 14.2 %all_to_all.10.got = f32[16,3,4,128]{3,2,1,0:T(4,128)S(1)} all-to-all(f32[16,3,4,128]{3,2,1,0:T(4,128)S(1)} %get-tuple-element.18), channel_id=1, replica_groups=mesh['cases'=2,'circ'=4,'lat'=4] {'circ','lat'}, dimensions={0} | all-to-all | bytes 196608 | tf_op jit(solution)/shard_map/all_to_all | solution.py:498
  18.3 3.1 %solve_patch.1 = (f32[16,4,128]{2,1,0:T(4,128)S(1)}, f32[4,128]{1,0:T(4,128)}) custom-call(f32[16,3,4,128]{3,2,1,0:T(4,128)S(1)} %all_to_all.10.got, f32[4,128]{1,0:T(4,128)S(1)} %get-tuple-element.19.road, s32[4,128]{1,0:T(4,128)S(1)} %get-tuple-element.20.active, f32[512,512]{1,0:T(8,128)S(1)} %get-tuple-element.21.block), custom_call_target="tpu_custom_call" | custom-call | tf_op jit(solution)/shard_map/solve_patch/pallas_call | solution.py:499
  21.4 9.2 %all_to_all.11.back = f32[16,4,128]{2,1,0:T(4,128)S(1)} all-to-all(f32[16,4,128]{2,1,0:T(4,128)S(1)} %get-tuple-element.22), channel_id=1, replica_groups=mesh['cases'=2,'circ'=4,'lat'=4] {'circ','lat'}, dimensions={0} | all-to-all | bytes 65536 | tf_op jit(solution)/shard_map/all_to_all | solution.py:516
  30.5 1.2 %finish_nodes.1 = f32[3,128,128]{2,1,0:T(8,128)} custom-call(f32[3,128,128]{2,1,0:T(8,128)S(1)} %get-tuple-element.13.trial, f32[3,128,128]{2,1,0:T(8,128)S(1)} %get-tuple-element.14.near, s32[8,128]{1,0:T(8,128)S(1)} %get-tuple-element.15.node, s32[8,128]{1,0:T(8,128)S(1)} %get-tuple-element.16.owner, s32[8,128]{1,0:T(8,128)S(1)} %get-tuple-element.17.slot, ...), custom_call_target="tpu_custom_call" | custom-call | tf_op jit(solution)/shard_map/finish_nodes/pallas_call | solution.py:517

commit v7 on v6

--- a/solution.py
+++ b/solution.py
@@ -310,7 +310,7 @@
 
 
 def solve_kernel(
-    lats, got, road, active, block, send, pressure, work, press, rowed, layered
+    lats, got, road, active, block, send, work, press, rowed, layered
 ):
     size = 4 * LANES
     mask, rhs, soft = patch_system(lats, got, road, active, rowed, layered)
@@ -350,7 +350,6 @@
         press[...] = x
         for j in range(4):
             part = x[:, j * LANES : (j + 1) * LANES]
-            pressure[j : j + 1, :] = part
             send[:, j, :] = jnp.broadcast_to(part, (send.shape[0], LANES))
 
     def gap(x):
@@ -389,7 +388,7 @@
             finish(lax.fori_loop(0, 2, refine, zero))
 
 
-def finish_kernel(axes, trial, near, node, owner, slot, got, back, out):
+def finish_kernel(axes, trial, near, node, owner, slot, got, back, out, pressure):
     circs, lats = axes
     owners = got.shape[0]
     rows, cols = trial.shape[1:]
@@ -413,6 +412,7 @@
         )
         out[c] = trial[c] + (kc * circ_in + kl * lat_in) / diag_k
 
+    pressure[...] = back[me]
     answers = jnp.concatenate([back[:, j, :] for j in range(4)], axis=0)
     answers = jnp.concatenate(thirds(answers), axis=1).astype(BF16)
     step = 2 if chunks % 2 == 0 else 1
@@ -496,14 +496,11 @@
         ]
     )
     got = lax.all_to_all(send, ("circ", "lat"), split_axis=0, concat_axis=0, tiled=True)
-    reply, pressure = pl.pallas_call(
+    reply = pl.pallas_call(
         functools.partial(solve_kernel, lats),
         in_specs=[block] * 4,
-        out_specs=[block, block],
-        out_shape=[
-            jax.ShapeDtypeStruct((owners,) + strip, F32),
-            jax.ShapeDtypeStruct(strip, F32),
-        ],
+        out_specs=block,
+        out_shape=jax.ShapeDtypeStruct((owners,) + strip, F32),
         scratch_shapes=[
             pltpu.VMEM((size, size + LANES), F32),
             pltpu.VMEM((1, size), F32),
@@ -514,11 +511,14 @@
         name="solve_patch",
     )(got, roads, actives, blocks)
     back = lax.all_to_all(reply, ("circ", "lat"), split_axis=0, concat_axis=0, tiled=True)
-    new_disp = pl.pallas_call(
+    new_disp, pressure = pl.pallas_call(
         functools.partial(finish_kernel, (circs, lats)),
         in_specs=[block] * 7,
-        out_specs=block,
-        out_shape=jax.ShapeDtypeStruct(disp.shape, F32),
+        out_specs=[block, block],
+        out_shape=[
+            jax.ShapeDtypeStruct(disp.shape, F32),
+            jax.ShapeDtypeStruct(strip, F32),
+        ],
         compiler_params=params,
         name="finish_nodes",
     )(trial, near, nodes, owner, slots, got, back)

time: 32 us -> 31.5 us (0.984)
  Pallas kernels: 6.53 us -> 5.95 us
    pallas_call x1, Pallas kernels: 3.12 us -> 2.53 us  [shards(): pl.pallas_call(functools.partial(solve_kernel, lats), in_specs=[block] *...]
where the time goes in v7:
time: 31.5 us; the launch traced here: 31.2 us
  blocking collectives  23.3 us (74%)
  Pallas kernels  5.95 us (19%)
  between operations  1.94 us (6%)
    all_to_all x1, blocking collectives, shards(): lax.all_to_all(send, ('circ', 'lat'), split_axis=0, concat_axis=0, tiled=...  14.2 us
    all_to_all x1, blocking collectives, shards(): lax.all_to_all(reply, ('circ', 'lat'), split_axis=0, concat_axis=0, tiled...  9.16 us
    pallas_call x1, Pallas kernels, shards(): pl.pallas_call(functools.partial(solve_kernel, lats), in_specs=[block] *...  2.53 us
    pallas_call x1, Pallas kernels, shards(): pl.pallas_call(functools.partial(pack_kernel, (circs, lats)), in_specs=[p...  2.17 us
    pallas_call x1, Pallas kernels, shards(): pl.pallas_call(functools.partial(finish_kernel, (circs, lats)), in_specs=...  1.25 us

profile of v7, /device:TPU:0, one launch (start us, length us, event | category | flops | bytes accessed | tf_op | source)
XLA Modules:
  0.0 31.2 jit_solution(17553513153667901018)
XLA Ops:
  1.9 2.2 %pack_rows.1 = (f32[16,3,4,128]{3,2,1,0:T(4,128)S(1)}, f32[3,128,128]{2,1,0:T(8,128)S(1)}, f32[3,128,128]{2,1,0:T(8,128)S(1)}, s32[8,128]{1,0:T(8,128)S(1)}, s32...) custom-call(s32[1]{0:T(128)S(6)} %copy.14.count, ...), custom_call_target="tpu_custom_call" | custom-call | tf_op jit(solution)/shard_map/pack_rows/pallas_call | solution.py:465
  4.1 14.2 %all_to_all.10.got = f32[16,3,4,128]{3,2,1,0:T(4,128)S(1)} all-to-all(f32[16,3,4,128]{3,2,1,0:T(4,128)S(1)} %get-tuple-element.18), channel_id=1, replica_groups=mesh['cases'=2,'circ'=4,'lat'=4] {'circ','lat'}, dimensions={0} | all-to-all | bytes 196608 | tf_op jit(solution)/shard_map/all_to_all | solution.py:498
  18.3 2.5 %solve_patch.1 = f32[16,4,128]{2,1,0:T(4,128)S(1)} custom-call(f32[16,3,4,128]{3,2,1,0:T(4,128)S(1)} %all_to_all.10.got, f32[4,128]{1,0:T(4,128)S(1)} %get-tuple-element.19.road, s32[4,128]{1,0:T(4,128)S(1)} %get-tuple-element.20.active, f32[512,512]{1,0:T(8,128)S(1)} %get-tuple-element.21.block), custom_call_target="tpu_custom_call" | custom-call | tf_op jit(solution)/shard_map/solve_patch/pallas_call | solution.py:499
  20.8 9.2 %all_to_all.11.back = f32[16,4,128]{2,1,0:T(4,128)S(1)} all-to-all(f32[16,4,128]{2,1,0:T(4,128)S(1)} %solve_patch.1), channel_id=1, replica_groups=mesh['cases'=2,'circ'=4,'lat'=4] {'circ','lat'}, dimensions={0} | all-to-all | bytes 65536 | tf_op jit(solution)/shard_map/all_to_all | solution.py:513
  30.0 1.3 %finish_nodes.1 = (f32[3,128,128]{2,1,0:T(8,128)}, f32[4,128]{1,0:T(4,128)}) custom-call(f32[3,128,128]{2,1,0:T(8,128)S(1)} %get-tuple-element.13.trial, f32[3,128,128]{2,1,0:T(8,128)S(1)} %get-tuple-element.14.near, s32[8,128]{1,0:T(8,128)S(1)} %get-tuple-element.15.node, s32[8,128]{1,0:T(8,128)S(1)} %get-tuple-element.16.owner, ...), custom_call_target="tpu_custom_call" | custom-call | tf_op jit(solution)/shard_map/finish_nodes/pallas_call | solution.py:514

commit v8 on v7

--- a/solution.py
+++ b/solution.py
@@ -15,6 +15,7 @@
 CG_AGAIN = 4
 CG_STEPS = 40
 CG_STOP = 2e-14
+FIRST_STOP = 1e-12
 TRUE_STOP = 4e-13
 
 
@@ -355,8 +356,8 @@
     def gap(x):
         return rhs - times(block, x, mask, soft)
 
-    def small(r):
-        return dot(r, scale * r)[0, 0] <= TRUE_STOP * start[0, 0]
+    def small(r, bound):
+        return dot(r, scale * r)[0, 0] <= bound * start[0, 0]
 
     state = begin(zero, rhs)
     for _ in range(CG_FIRST):
@@ -367,7 +368,7 @@
     first, rest = state[:2]
     finish(first)
 
-    @pl.when(jnp.logical_not(small(rest)))
+    @pl.when(jnp.logical_not(small(rest, FIRST_STOP)))
     def _():
         def going(state):
             step, norm = state[0], state[9]
@@ -379,7 +380,7 @@
         x = lax.while_loop(going, body, (0,) + begin(first, gap(first)))[1]
         finish(x)
 
-        @pl.when(jnp.logical_not(small(gap(x))))
+        @pl.when(jnp.logical_not(small(gap(x), TRUE_STOP)))
         def _():
             def refine(step, x):
                 factor_solve(block, mask, gap(x), soft, work, press)

time: 31.5 us -> 31.5 us (level)
  no operation moved by 1% of the time
where the time goes in v8:
time: 31.5 us; the launch traced here: 31.2 us
  blocking collectives  23.3 us (74%)
  Pallas kernels  5.95 us (19%)
  between operations  1.94 us (6%)
    all_to_all x1, blocking collectives, shards(): lax.all_to_all(send, ('circ', 'lat'), split_axis=0, concat_axis=0, tiled=...  14.2 us
    all_to_all x1, blocking collectives, shards(): lax.all_to_all(reply, ('circ', 'lat'), split_axis=0, concat_axis=0, tiled...  9.16 us
    pallas_call x1, Pallas kernels, shards(): pl.pallas_call(functools.partial(solve_kernel, lats), in_specs=[block] *...  2.53 us
    pallas_call x1, Pallas kernels, shards(): pl.pallas_call(functools.partial(pack_kernel, (circs, lats)), in_specs=[p...  2.17 us
    pallas_call x1, Pallas kernels, shards(): pl.pallas_call(functools.partial(finish_kernel, (circs, lats)), in_specs=...  1.25 us

profile of v8, /device:TPU:0, one launch (start us, length us, event | category | flops | bytes accessed | tf_op | source)
XLA Modules:
  0.0 31.2 jit_solution(17558072506858186691)
XLA Ops:
  1.9 2.2 %pack_rows.1 = (f32[16,3,4,128]{3,2,1,0:T(4,128)S(1)}, f32[3,128,128]{2,1,0:T(8,128)S(1)}, f32[3,128,128]{2,1,0:T(8,128)S(1)}, s32[8,128]{1,0:T(8,128)S(1)}, s32...) custom-call(s32[1]{0:T(128)S(6)} %copy.14.count, ...), custom_call_target="tpu_custom_call" | custom-call | tf_op jit(solution)/shard_map/pack_rows/pallas_call | solution.py:466
  4.1 14.2 %all_to_all.10.got = f32[16,3,4,128]{3,2,1,0:T(4,128)S(1)} all-to-all(f32[16,3,4,128]{3,2,1,0:T(4,128)S(1)} %get-tuple-element.18), channel_id=1, replica_groups=mesh['cases'=2,'circ'=4,'lat'=4] {'circ','lat'}, dimensions={0} | all-to-all | bytes 196608 | tf_op jit(solution)/shard_map/all_to_all | solution.py:499
  18.3 2.5 %solve_patch.1 = f32[16,4,128]{2,1,0:T(4,128)S(1)} custom-call(f32[16,3,4,128]{3,2,1,0:T(4,128)S(1)} %all_to_all.10.got, f32[4,128]{1,0:T(4,128)S(1)} %get-tuple-element.19.road, s32[4,128]{1,0:T(4,128)S(1)} %get-tuple-element.20.active, f32[512,512]{1,0:T(8,128)S(1)} %get-tuple-element.21.block), custom_call_target="tpu_custom_call" | custom-call | tf_op jit(solution)/shard_map/solve_patch/pallas_call | solution.py:500
  20.8 9.2 %all_to_all.11.back = f32[16,4,128]{2,1,0:T(4,128)S(1)} all-to-all(f32[16,4,128]{2,1,0:T(4,128)S(1)} %solve_patch.1), channel_id=1, replica_groups=mesh['cases'=2,'circ'=4,'lat'=4] {'circ','lat'}, dimensions={0} | all-to-all | bytes 65536 | tf_op jit(solution)/shard_map/all_to_all | solution.py:514
  30.0 1.3 %finish_nodes.1 = (f32[3,128,128]{2,1,0:T(8,128)}, f32[4,128]{1,0:T(4,128)}) custom-call(f32[3,128,128]{2,1,0:T(8,128)S(1)} %get-tuple-element.13.trial, f32[3,128,128]{2,1,0:T(8,128)S(1)} %get-tuple-element.14.near, s32[8,128]{1,0:T(8,128)S(1)} %get-tuple-element.15.node, s32[8,128]{1,0:T(8,128)S(1)} %get-tuple-element.16.owner, ...), custom_call_target="tpu_custom_call" | custom-call | tf_op jit(solution)/shard_map/finish_nodes/pallas_call | solution.py:515

commit v9 on v8

--- a/solution.py
+++ b/solution.py
@@ -143,9 +143,9 @@
     )
     part = [spread[i * owners : (i + 1) * owners] for i in range(13)]
     for v in range(3):
-        send[:, 0, v, :] = part[3 * v] + part[3 * v + 1] + part[3 * v + 2]
-    send[:, 0, 3, :] = part[9] + part[10]
-    send[:, 2, 0, :] = part[11] + part[12]
+        send[:, v, 0, :] = part[3 * v] + part[3 * v + 1] + part[3 * v + 2]
+    send[:, 3, 0, :] = part[9] + part[10]
+    send[:, 8, 0, :] = part[11] + part[12]
 
     my_circ, my_lat = lax.axis_index("circ"), lax.axis_index("lat")
     me = my_circ * lats + my_lat
@@ -156,13 +156,14 @@
     device = iota((owners, LANES), 0)
     for c in range(3):
         layers = edges(u[c])
+        if c == 2:
+            for t, layer in enumerate(layers):
+                send[:, 4 + t, 0, :] = jnp.broadcast_to(layer, (owners, LANES))
+            continue
         lacks = jnp.zeros((owners, LANES), F32)
         for layer, reader in zip(layers, (prior, after, west, east)):
             lacks = jnp.where(device == reader, layer, lacks)
-        send[:, 2, 1 + c, :] = lacks
-        if c == 2:
-            for t, layer in enumerate(layers):
-                send[:, 1, t, :] = jnp.broadcast_to(layer, (owners, LANES))
+        send[:, 9 + c, 0, :] = lacks
     for copy in copies[6:]:
         copy.wait()
 
@@ -179,8 +180,8 @@
     total = jnp.zeros((4 * group, LANES), F32)
     for first in range(0, owners, group):
         some = slice(first, first + group)
-        w, kc, kl, node = [got[some, 0, v, :] for v in range(4)]
-        slot = got[some, 2, 0, :].astype(I32)
+        w, kc, kl, node = [got[some, v, 0, :] for v in range(4)]
+        slot = got[some, 8, 0, :].astype(I32)
         node = node.astype(I32)
         lat = node & (cols - 1)
         sender = jnp.where(kc > 0.0, iota(kc.shape, 0) + first, 0)
@@ -235,7 +236,7 @@
         jnp.where((lat == 0) & (side > 0), sender - 1 + 3 * owners, -1),
     )
     for t in range(4):
-        layered[t] = got[:, 1, t, :]
+        layered[t] = got[:, 4 + t, 0, :]
     layers = layered[...].reshape(owners * 4, LANES)
     layers = jnp.concatenate(thirds(layers), axis=1).astype(BF16)
 
@@ -403,8 +404,10 @@
     kc, kl, diag_k = near[0], near[1], near[2]
     row, col = iota((rows, cols), 0), iota((rows, cols), 1)
     for c in range(3):
-        down, up = got[after, 2, 1 + c : 2 + c, :], got[before, 2, 1 + c : 2 + c, :]
-        east, west = got[right_dev, 2, 1 + c : 2 + c, :], got[left_dev, 2, 1 + c : 2 + c, :]
+        rows_at = (9 + c,) * 4 if c < 2 else (4, 5, 6, 7)
+        down, up, east, west = [
+            got[device, at] for device, at in zip((after, before, right_dev, left_dev), rows_at)
+        ]
         east = jnp.where(my_lat < lats - 1, east, 0.0)
         west = jnp.where(my_lat > 0, west, 0.0)
         circ_in = jnp.where(row == rows - 1, down, jnp.where(row == 0, up, 0.0))
@@ -468,7 +471,7 @@
         in_specs=[pl.BlockSpec(memory_space=pltpu.SMEM)] * 2 + [anywhere] * 9,
         out_specs=[block] * 9,
         out_shape=[
-            jax.ShapeDtypeStruct((owners, 3, 4, LANES), F32),
+            jax.ShapeDtypeStruct((owners, 11, 1, LANES), F32),
             jax.ShapeDtypeStruct((3, rows, cols), F32),
             jax.ShapeDtypeStruct((3, rows, cols), F32),
             listed,

time: 31.5 us -> 31.3 us (level)
  no operation moved by 1% of the time
where the time goes in v9:
time: 31.3 us; the launch traced here: 31 us
  blocking collectives  23.2 us (74%)
  Pallas kernels  5.94 us (19%)
  between operations  1.94 us (6%)
    all_to_all x1, blocking collectives, shards(): lax.all_to_all(send, ('circ', 'lat'), split_axis=0, concat_axis=0, tiled=...  14.1 us
    all_to_all x1, blocking collectives, shards(): lax.all_to_all(reply, ('circ', 'lat'), split_axis=0, concat_axis=0, tiled...  9.09 us
    pallas_call x1, Pallas kernels, shards(): pl.pallas_call(functools.partial(solve_kernel, lats), in_specs=[block] *...  2.52 us
    pallas_call x1, Pallas kernels, shards(): pl.pallas_call(functools.partial(pack_kernel, (circs, lats)), in_specs=[p...  2.17 us
    pallas_call x1, Pallas kernels, shards(): pl.pallas_call(functools.partial(finish_kernel, (circs, lats)), in_specs=...  1.25 us

profile of v9, /device:TPU:0, one launch (start us, length us, event | category | flops | bytes accessed | tf_op | source)
XLA Modules:
  0.0 31.0 jit_solution(5652850768551484687)
XLA Ops:
  1.9 2.2 %pack_rows.1 = (f32[16,11,1,128]{3,2,1,0:T(1,128)S(1)}, f32[3,128,128]{2,1,0:T(8,128)S(1)}, f32[3,128,128]{2,1,0:T(8,128)S(1)}, s32[8,128]{1,0:T(8,128)S(1)}, s3...) custom-call(s32[1]{0:T(128)S(6)} %copy.14.count, ...), custom_call_target="tpu_custom_call" | custom-call | tf_op jit(solution)/shard_map/pack_rows/pallas_call | solution.py:469
  4.1 14.1 %all_to_all.10.got = f32[16,11,1,128]{3,2,1,0:T(1,128)S(1)} all-to-all(f32[16,11,1,128]{3,2,1,0:T(1,128)S(1)} %get-tuple-element.18), channel_id=1, replica_groups=mesh['cases'=2,'circ'=4,'lat'=4] {'circ','lat'}, dimensions={0} | all-to-all | bytes 180224 | tf_op jit(solution)/shard_map/all_to_all | solution.py:502
  18.2 2.5 %solve_patch.1 = f32[16,4,128]{2,1,0:T(4,128)S(1)} custom-call(f32[16,11,1,128]{3,2,1,0:T(1,128)S(1)} %all_to_all.10.got, f32[4,128]{1,0:T(4,128)S(1)} %get-tuple-element.19.road, s32[4,128]{1,0:T(4,128)S(1)} %get-tuple-element.20.active, f32[512,512]{1,0:T(8,128)S(1)} %get-tuple-element.21.block), custom_call_target="tpu_custom_call" | custom-call | tf_op jit(solution)/shard_map/solve_patch/pallas_call | solution.py:503
  20.7 9.1 %all_to_all.11.back = f32[16,4,128]{2,1,0:T(4,128)S(1)} all-to-all(f32[16,4,128]{2,1,0:T(4,128)S(1)} %solve_patch.1), channel_id=1, replica_groups=mesh['cases'=2,'circ'=4,'lat'=4] {'circ','lat'}, dimensions={0} | all-to-all | bytes 65536 | tf_op jit(solution)/shard_map/all_to_all | solution.py:517
  29.8 1.3 %finish_nodes.1 = (f32[3,128,128]{2,1,0:T(8,128)}, f32[4,128]{1,0:T(4,128)}) custom-call(f32[3,128,128]{2,1,0:T(8,128)S(1)} %get-tuple-element.13.trial, f32[3,128,128]{2,1,0:T(8,128)S(1)} %get-tuple-element.14.near, s32[8,128]{1,0:T(8,128)S(1)} %get-tuple-element.15.node, s32[8,128]{1,0:T(8,128)S(1)} %get-tuple-element.16.owner, ...), custom_call_target="tpu_custom_call" | custom-call | tf_op jit(solution)/shard_map/finish_nodes/pallas_call | solution.py:518

commit v10 on v9

--- a/solution.py
+++ b/solution.py
@@ -58,7 +58,7 @@
 
 def pack_kernel(
     axes, count, spin, node, dest, slot, stiff, disp, load, road, active, block,
-    send, trial, near, nodes, owner, slots, roads, actives, blocks,
+    send, trial, near, nodes, owner, slots, roads, actives, blocks, late,
     u, springs, loads, dests, sems,
 ):
     circs, lats = axes
@@ -163,7 +163,7 @@
         lacks = jnp.zeros((owners, LANES), F32)
         for layer, reader in zip(layers, (prior, after, west, east)):
             lacks = jnp.where(device == reader, layer, lacks)
-        send[:, 9 + c, 0, :] = lacks
+        late[c] = lacks
     for copy in copies[6:]:
         copy.wait()
 
@@ -312,9 +312,11 @@
 
 
 def solve_kernel(
-    lats, got, road, active, block, send, work, press, rowed, layered
+    lats, got, road, active, block, late, send, work, press, rowed, layered
 ):
     size = 4 * LANES
+    for c in range(2):
+        send[:, 4 + c, 0, :] = late[c]
     mask, rhs, soft = patch_system(lats, got, road, active, rowed, layered)
     square = iota((LANES, LANES), 0) == iota((LANES, LANES), 1)
     diagonal = jnp.concatenate(
@@ -352,7 +354,7 @@
         press[...] = x
         for j in range(4):
             part = x[:, j * LANES : (j + 1) * LANES]
-            send[:, j, :] = jnp.broadcast_to(part, (send.shape[0], LANES))
+            send[:, j, 0, :] = jnp.broadcast_to(part, (send.shape[0], LANES))
 
     def gap(x):
         return rhs - times(block, x, mask, soft)
@@ -404,9 +406,10 @@
     kc, kl, diag_k = near[0], near[1], near[2]
     row, col = iota((rows, cols), 0), iota((rows, cols), 1)
     for c in range(3):
-        rows_at = (9 + c,) * 4 if c < 2 else (4, 5, 6, 7)
+        source = back if c < 2 else got
+        rows_at = (4 + c,) * 4 if c < 2 else (4, 5, 6, 7)
         down, up, east, west = [
-            got[device, at] for device, at in zip((after, before, right_dev, left_dev), rows_at)
+            source[device, at] for device, at in zip((after, before, right_dev, left_dev), rows_at)
         ]
         east = jnp.where(my_lat < lats - 1, east, 0.0)
         west = jnp.where(my_lat > 0, west, 0.0)
@@ -416,8 +419,9 @@
         )
         out[c] = trial[c] + (kc * circ_in + kl * lat_in) / diag_k
 
-    pressure[...] = back[me]
-    answers = jnp.concatenate([back[:, j, :] for j in range(4)], axis=0)
+    for j in range(4):
+        pressure[j : j + 1, :] = back[me, j]
+    answers = jnp.concatenate([back[:, j, 0, :] for j in range(4)], axis=0)
     answers = jnp.concatenate(thirds(answers), axis=1).astype(BF16)
     step = 2 if chunks % 2 == 0 else 1
     span = step * LANES
@@ -466,12 +470,12 @@
     lists = [x.reshape(-1, LANES) for x in (foot_node, foot_dest, foot_slot)]
     listed = jax.ShapeDtypeStruct(lists[0].shape, I32)
     strip = (4, LANES)
-    send, trial, near, nodes, owner, slots, roads, actives, blocks = pl.pallas_call(
+    send, trial, near, nodes, owner, slots, roads, actives, blocks, late = pl.pallas_call(
         functools.partial(pack_kernel, (circs, lats)),
         in_specs=[pl.BlockSpec(memory_space=pltpu.SMEM)] * 2 + [anywhere] * 9,
-        out_specs=[block] * 9,
+        out_specs=[block] * 10,
         out_shape=[
-            jax.ShapeDtypeStruct((owners, 11, 1, LANES), F32),
+            jax.ShapeDtypeStruct((owners, 9, 1, LANES), F32),
             jax.ShapeDtypeStruct((3, rows, cols), F32),
             jax.ShapeDtypeStruct((3, rows, cols), F32),
             listed,
@@ -480,6 +484,7 @@
             jax.ShapeDtypeStruct(strip, F32),
             jax.ShapeDtypeStruct(strip, I32),
             jax.ShapeDtypeStruct((size, size), F32),
+            jax.ShapeDtypeStruct((2, owners, LANES), F32),
         ],
         scratch_shapes=[
             pltpu.VMEM((3, rows, cols), F32),
@@ -502,9 +507,9 @@
     got = lax.all_to_all(send, ("circ", "lat"), split_axis=0, concat_axis=0, tiled=True)
     reply = pl.pallas_call(
         functools.partial(solve_kernel, lats),
-        in_specs=[block] * 4,
+        in_specs=[block] * 5,
         out_specs=block,
-        out_shape=jax.ShapeDtypeStruct((owners,) + strip, F32),
+        out_shape=jax.ShapeDtypeStruct((owners, 6, 1, LANES), F32),
         scratch_shapes=[
             pltpu.VMEM((size, size + LANES), F32),
             pltpu.VMEM((1, size), F32),
@@ -513,7 +518,7 @@
         ],
         compiler_params=params,
         name="solve_patch",
-    )(got, roads, actives, blocks)
+    )(got, roads, actives, blocks, late)
     back = lax.all_to_all(reply, ("circ", "lat"), split_axis=0, concat_axis=0, tiled=True)
     new_disp, pressure = pl.pallas_call(
         functools.partial(finish_kernel, (circs, lats)),

time: 31.3 us -> 31.2 us (level)
  no operation moved by 1% of the time
where the time goes in v10:
time: 31.2 us; the launch traced here: 30.9 us
  blocking collectives  23 us (74%)
  Pallas kernels  5.95 us (19%)
  between operations  1.94 us (6%)
    all_to_all x1, blocking collectives, shards(): lax.all_to_all(send, ('circ', 'lat'), split_axis=0, concat_axis=0, tiled=...  13.9 us
    all_to_all x1, blocking collectives, shards(): lax.all_to_all(reply, ('circ', 'lat'), split_axis=0, concat_axis=0, tiled...  9.12 us
    pallas_call x1, Pallas kernels, shards(): pl.pallas_call(functools.partial(solve_kernel, lats), in_specs=[block] *...  2.53 us
    pallas_call x1, Pallas kernels, shards(): pl.pallas_call(functools.partial(pack_kernel, (circs, lats)), in_specs=[p...  2.17 us
    pallas_call x1, Pallas kernels, shards(): pl.pallas_call(functools.partial(finish_kernel, (circs, lats)), in_specs=...  1.25 us

profile of v10, /device:TPU:0, one launch (start us, length us, event | category | flops | bytes accessed | tf_op | source)
XLA Modules:
  0.0 30.9 jit_solution(6187090050018867761)
XLA Ops:
  1.9 2.2 %pack_rows.1 = (f32[16,9,1,128]{3,2,1,0:T(1,128)S(1)}, f32[3,128,128]{2,1,0:T(8,128)S(1)}, f32[3,128,128]{2,1,0:T(8,128)S(1)}, s32[8,128]{1,0:T(8,128)S(1)}, s32...) custom-call(s32[1]{0:T(128)S(6)} %copy.14.count, ...), custom_call_target="tpu_custom_call" | custom-call | tf_op jit(solution)/shard_map/pack_rows/pallas_call | solution.py:473
  4.1 13.9 %all_to_all.10.got = f32[16,9,1,128]{3,2,1,0:T(1,128)S(1)} all-to-all(f32[16,9,1,128]{3,2,1,0:T(1,128)S(1)} %get-tuple-element.19), channel_id=1, replica_groups=mesh['cases'=2,'circ'=4,'lat'=4] {'circ','lat'}, dimensions={0} | all-to-all | bytes 147456 | tf_op jit(solution)/shard_map/all_to_all | solution.py:507
  18.0 2.5 %solve_patch.1 = f32[16,6,1,128]{3,2,1,0:T(1,128)S(1)} custom-call(f32[16,9,1,128]{3,2,1,0:T(1,128)S(1)} %all_to_all.10.got, f32[4,128]{1,0:T(4,128)S(1)} %get-tuple-element.20.road, s32[4,128]{1,0:T(4,128)S(1)} %get-tuple-element.21.active, f32[512,512]{1,0:T(8,128)S(1)} %get-tuple-element.22.block, f32[2,16,128]{2,1,0:T(8,128)S(1)} %get-tuple-element.23.late), custom_call_target="tpu_custom_call" | custom-call | tf_op jit(solution)/shard_map/solve_patch/pallas_call | solution.py:508
  20.5 9.1 %all_to_all.11.back = f32[16,6,1,128]{3,2,1,0:T(1,128)S(1)} all-to-all(f32[16,6,1,128]{3,2,1,0:T(1,128)S(1)} %solve_patch.1), channel_id=1, replica_groups=mesh['cases'=2,'circ'=4,'lat'=4] {'circ','lat'}, dimensions={0} | all-to-all | bytes 98304 | tf_op jit(solution)/shard_map/all_to_all | solution.py:522
  29.6 1.2 %finish_nodes.1 = (f32[3,128,128]{2,1,0:T(8,128)}, f32[4,128]{1,0:T(4,128)}) custom-call(f32[3,128,128]{2,1,0:T(8,128)S(1)} %get-tuple-element.14.trial, f32[3,128,128]{2,1,0:T(8,128)S(1)} %get-tuple-element.15.near, s32[8,128]{1,0:T(8,128)S(1)} %get-tuple-element.16.node, s32[8,128]{1,0:T(8,128)S(1)} %get-tuple-element.17.owner, ...), custom_call_target="tpu_custom_call" | custom-call | tf_op jit(solution)/shard_map/finish_nodes/pallas_call | solution.py:523
